TPU v7x, 32 devices: a whole 2x2x4 slice. The times are simulated.
32 devices in a mesh: region: 4 (over z), gx: 4 (over y, x), gy: 2 (over core).
Axes of the slice: x: 2, y: 2, z: 4, core: 2. Of those that a mesh axis runs over, the one named last changes fastest.
Arguments:
- spins: float32 [3, 8, 128, 256], P(None, 'region', 'gx', 'gy'), may hold values from -1 to 1, as said below
- uniforms: float32 [2, 8, 128, 256], P(None, 'region', 'gx', 'gy'), may hold values from 0 to 1
- trials: float32 [2, 3, 8, 128, 256], P(None, None, 'region', 'gx', 'gy'), may hold values from -1 to 1
- exch_kernel: float32 [3, 3, 3], replicated, may hold values from -0.5 to 1
- film_m: float32 [3, 2048, 512], P(None, ('region', 'gx'), 'gy'), may hold values from -1 to 1, as said below
- film_anis: float32 [2048, 512], P(('region', 'gx'), 'gy'), may hold values from 0.2 to 2
Outputs:
- spins_out: float32 [3, 8, 128, 256], P(None, 'region', 'gx', 'gy')
- film_out: float32 [3, 2048, 512], P(None, ('region', 'gx'), 'gy')
Inputs may be any that keep to these rules, and one draw needn't show every extreme that they name: `spins`: the three components of each site form a unit vector. `film_m`: the three components of each cell form a unit vector.
All inputs are finite; a program needn't handle non-finite values.
Results may differ from a plain program's by a relative error of at most 0.0001.
Values sent between devices are 32-bit elements; how exact they have to be, the bound alone decides.
A program may use at most 64 MiB of HBM per device.

v0:
```python
import jax
import jax.numpy as jnp
from jax import lax
from jax.sharding import PartitionSpec as P

K = 8
SWEEPS = 2


coupling_down = 1.0
anisotropy = 0.5
inverse_temp = 2.0
softness = 0.05
step_cone = 0.4
coupling_up = 2.0
damping = 0.1
time_step = 0.05


def extended(cells, sides, width):
    for axis, dim in sides:
        count = lax.axis_size(axis)
        ends = count - 1
        head = lax.slice_in_dim(cells, 0, width, axis=dim)
        tail = lax.slice_in_dim(cells, cells.shape[dim] - width, cells.shape[dim], axis=dim)
        cells = jnp.concatenate(
            [
                lax.ppermute(tail, axis, [(i, (i + 1) % count) for i in range(ends)]),
                cells,
                lax.ppermute(head, axis, [((i + 1) % count, i) for i in range(ends)]),
            ],
            axis=dim,
        )
    return cells


def spread(value, axis, source):
    kept = jnp.where(lax.axis_index(axis) == source, value, 0).astype(value.dtype)
    return lax.psum(kept, axis)


def normalized(vector):
    return vector / jnp.sqrt(jnp.sum(vector * vector, axis=0, keepdims=True))


def apply_kernel(matrix, vector):
    return jnp.stack(
        [
            matrix[component, 0] * vector[0]
            + matrix[component, 1] * vector[1]
            + matrix[component, 2] * vector[2]
            for component in range(3)
        ]
    )


def apply_transposed(matrix, vector):
    return jnp.stack(
        [
            matrix[0, component] * vector[0]
            + matrix[1, component] * vector[1]
            + matrix[2, component] * vector[2]
            for component in range(3)
        ]
    )


def local_field(padded, exch_kernel):
    forward = (padded[:, 2:, 1:-1, 1:-1], padded[:, 1:-1, 2:, 1:-1], padded[:, 1:-1, 1:-1, 2:])
    backward = (padded[:, :-2, 1:-1, 1:-1], padded[:, 1:-1, :-2, 1:-1], padded[:, 1:-1, 1:-1, :-2])
    summed = apply_kernel(exch_kernel[0], forward[0]) + apply_transposed(
        exch_kernel[0], backward[0]
    )
    for direction in (1, 2):
        summed = summed + apply_kernel(exch_kernel[direction], forward[direction])
        summed = summed + apply_transposed(exch_kernel[direction], backward[direction])
    return summed


def metropolis(spins, padded, exch_kernel, film_near, trial_move, uniform_draw, colour_mask):
    field_sum = local_field(padded, exch_kernel) + coupling_down * film_near
    proposal = normalized(spins + step_cone * trial_move)
    change = -jnp.sum((proposal - spins) * field_sum, axis=0) - anisotropy * (
        proposal[2] * proposal[2] - spins[2] * spins[2]
    )
    accept = jnp.exp(jnp.minimum(-inverse_temp * change, 0.0))
    weight = jax.nn.sigmoid((accept - uniform_draw) / softness)
    blended = normalized((1.0 - weight) * spins + weight * proposal)
    return jnp.where(colour_mask[None], blended, spins)


def cross_product(left, right):
    return jnp.stack(
        [
            left[1] * right[2] - left[2] * right[1],
            left[2] * right[0] - left[0] * right[2],
            left[0] * right[1] - left[1] * right[0],
        ]
    )


def film_rate(magnet, padded, film_anis, interface):
    laplace_sum = (
        padded[:, 2:, 1:-1]
        + padded[:, :-2, 1:-1]
        + padded[:, 1:-1, 2:]
        + padded[:, 1:-1, :-2]
        - 4.0 * magnet
    )
    field_sum = laplace_sum + coupling_up * interface
    field_sum = jnp.stack([field_sum[0], field_sum[1], field_sum[2] + film_anis * magnet[2]])
    precession = cross_product(magnet, field_sum)
    relaxation = cross_product(magnet, precession)
    return -(precession + damping * relaxation) / (1.0 + damping * damping)


def film_halo(magnet):
    return extended(magnet, ((("region", "gx"), 1), ("gy", 2)), 1)


def body(spins, uniforms, trials, exch_kernel, film_m, film_anis):
    layers_dev = spins.shape[1]
    rows_x = spins.shape[2]
    rows_y = spins.shape[3]
    piece_x = rows_x // K
    piece_y = rows_y // K
    gx_count = lax.axis_size("gx")
    gy_count = lax.axis_size("gy")
    region_pos = lax.axis_index("region")
    gx_pos = lax.axis_index("gx")
    gy_pos = lax.axis_index("gy")
    first_tile = (region_pos == 0) & (gx_pos == 0) & (gy_pos == 0)
    film_block = film_m[:, : piece_x * gx_count, : piece_y * gy_count]
    stack_spins, unif_all, trial_all = (spins, uniforms, trials)
    layer_pos = region_pos * layers_dev + jnp.arange(layers_dev, dtype=jnp.int32)
    film_block = spread(film_block, ("region", "gx", "gy"), 0)
    own_cells = lax.dynamic_slice(
        film_block, (jnp.int32(0), gx_pos * piece_x, gy_pos * piece_y), (3, piece_x, piece_y)
    )
    film_cells = jnp.repeat(jnp.repeat(own_cells, K, axis=1), K, axis=2)
    film_near = jnp.broadcast_to(film_cells[:, None], (3, stack_spins.shape[1], rows_x, rows_y))
    x_global = gx_pos * rows_x + jnp.arange(rows_x, dtype=jnp.int32)
    y_global = gy_pos * rows_y + jnp.arange(rows_y, dtype=jnp.int32)
    parity = (layer_pos[:, None, None] + x_global[None, :, None] + y_global[None, None, :]) % 2
    for sweep_index in range(SWEEPS):
        for colour in (0, 1):
            padded = extended(stack_spins, (("region", 1), ("gx", 2), ("gy", 3)), 1)
            stack_spins = metropolis(
                stack_spins,
                padded,
                exch_kernel,
                film_near,
                trial_all[sweep_index],
                unif_all[sweep_index],
                parity == colour,
            )
    averages = stack_spins[:, 0].reshape(3, piece_x, K, piece_y, K).mean(axis=(2, 4))
    gathered = lax.all_gather(averages[None], ("gx", "gy"), axis=0, tiled=True)
    assembled = (
        gathered.reshape(gx_count, gy_count, 3, piece_x, piece_y)
        .transpose(2, 0, 3, 1, 4)
        .reshape(3, gx_count * piece_x, gy_count * piece_y)
    )
    padded_block = jnp.pad(
        assembled,
        (
            (0, 0),
            (0, film_m.shape[1] - assembled.shape[1]),
            (0, film_m.shape[2] - assembled.shape[2]),
        ),
    )
    interface = jnp.where(first_tile, padded_block, 0.0)
    rate_start = film_rate(film_m, film_halo(film_m), film_anis, interface)
    predicted = film_m + time_step * rate_start
    rate_trial = film_rate(predicted, film_halo(predicted), film_anis, interface)
    corrected = film_m + 0.5 * time_step * (rate_start + rate_trial)
    return (stack_spins, normalized(corrected))


def solution(mesh):
    return jax.shard_map(
        body,
        mesh=mesh,
        in_specs=(
            P(None, "region", "gx", "gy"),
            P(None, "region", "gx", "gy"),
            P(None, None, "region", "gx", "gy"),
            P(),
            P(None, ("region", "gx"), "gy"),
            P(("region", "gx"), "gy"),
        ),
        out_specs=(P(None, "region", "gx", "gy"), P(None, ("region", "gx"), "gy")),
        check_vma=False,
    )
```

profile of v0, /device:TPU:0, one launch (start us, length us, event | category | flops | bytes accessed | tf_op | source)
XLA Modules:
  0.0 290.3 jit_solution(15975203236220558620)
XLA Ops:
  1.5 4.9 %collective-permute-start.1 = (f32[3,1,32,128]{3,2,1,0:T(8,128)S(1)}, f32[3,1,32,128]{3,2,1,0:T(8,128)S(1)}, u32[]{:S(2)}, u32[]{:S(2)}) collective-permute-start(f32[3,1,32,128]{3,2,1,0:T(8,128)S(1)} %get-tuple-element.224), channel_id=1, source_target_pairs={{0,8},{8,16},{16,24},{1,9},{9,17},{17,25},{2,10},{10,18},{18,26},{... | collective-permute-start | bytes 147464 | tf_op jit(solution)/shard_map/ppermute | solution.py:28
  9.1 41.8 %psum.7 = f32[3,16,32]{2,1,0:T(8,128)S(1)} all-reduce(f32[3,16,32]{2,1,0:T(8,128)S(1)} %slice_select_fusion), channel_id=1, replica_groups=mesh['region'=4,'gx'=4,'gy'=2] {'region','gx','gy'}, use_global_device_ids=true, to_apply=%region_1.2 | all-reduce | flops 1536 | bytes 12288 | tf_op jit(solution)/shard_map/psum | solution.py:39
  53.8 4.2 %collective-permute-start.3 = (f32[3,4,1,128]{3,2,1,0:T(1,128)S(1)}, f32[3,4,1,128]{3,2,1,0:T(1,128)S(1)}, u32[]{:S(2)}, u32[]{:S(2)}) collective-permute-start(f32[3,4,1,128]{3,2,1,0:T(1,128)S(1)} %get-tuple-element.150), channel_id=1, source_target_pairs={{0,2},{2,4},{4,6},{1,3},{3,5},{5,7},{8,10},{10,12},{12,14},{9,11},... | collective-permute-start | bytes 18440 | tf_op jit(solution)/shard_map/ppermute | solution.py:28
  59.3 5.5 %multiply_add_fusion.76 = (f32[1,2,32,128]{3,2,1,0:T(8,128)S(1)}, f32[1,2,32,128]{3,2,1,0:T(8,128)S(1)}, f32[1,2,32,128]{3,2,1,0:T(8,128)S(1)}) fusion(f32[3,3,32,128]{3,2,1,0:T(8,128)S(1)} %get-tuple-element.227, f32[]{:T(128)} %bitcast.4, f32[]{:T(128)} %bitcast.3, f32[]{:T(128)} %bitcast.2, f32[]{:T(128)} %bitcast.7, f32[]{:T(128)} %bitcast.6, ...), kind=kLoop, calls=%fused_computation.394 | loop fusion | flops 122880 | bytes 196644 | tf_op jit(solution)/shard_map/add | solution.py:49
  64.8 5.5 %multiply_add_fusion.73 = (f32[1,2,32,128]{3,2,1,0:T(8,128)S(1)}, f32[1,2,32,128]{3,2,1,0:T(8,128)S(1)}, f32[1,2,32,128]{3,2,1,0:T(8,128)S(1)}) fusion(f32[3,3,32,128]{3,2,1,0:T(8,128)S(1)} %get-tuple-element.214, f32[]{:T(128)} %bitcast.8, f32[]{:T(128)} %bitcast.5, f32[]{:T(128)} %bitcast.2, f32[]{:T(128)} %bitcast.9, f32[]{:T(128)} %bitcast.6, ...), kind=kLoop, calls=%fused_computation.391 | loop fusion | flops 122880 | bytes 196644 | tf_op jit(solution)/shard_map/add | solution.py:60
  78.0 3.8 %multiply_add_fusion.69 = (f32[1,2,32,128]{3,2,1,0:T(8,128)S(1)}, f32[1,2,32,128]{3,2,1,0:T(8,128)S(1)}) fusion(f32[1,2,32,128]{3,2,1,0:T(8,128)S(1)} %get-tuple-element.147, f32[1,2,32,128]{3,2,1,0:T(8,128)S(1)} %get-tuple-element.148, f32[1,2,32,128]{3,2,1,0:T(8,128)S(1)} %get-tuple-element.149, f32[]{:T(128)} %bitcast.17, f32[]{:T(128)} %bitcast.16, ...), kind=kLoop, calls=%fused_computation.387 | loop fusion | flops 81920 | bytes 163864 | tf_op jit(solution)/shard_map/add | solution.py:49
  87.5 3.8 %multiply_add_fusion.63 = (f32[1,2,32,128]{3,2,1,0:T(8,128)S(1)}, f32[1,2,32,128]{3,2,1,0:T(8,128)S(1)}) fusion(f32[1,2,32,128]{3,2,1,0:T(8,128)S(1)} %get-tuple-element.115, f32[1,2,32,128]{3,2,1,0:T(8,128)S(1)} %get-tuple-element.114, f32[1,2,32,128]{3,2,1,0:T(8,128)S(1)} %get-tuple-element.113, f32[]{:T(128)} %bitcast.27, f32[]{:T(128)} %bitcast.26, ...), kind=kLoop, calls=%fused_computation.381 | loop fusion | flops 81920 | bytes 163864 | tf_op jit(solution)/shard_map/add | solution.py:49
  93.3 3.8 %multiply_add_fusion.60 = (f32[1,2,32,128]{3,2,1,0:T(8,128)S(1)}, f32[1,2,32,128]{3,2,1,0:T(8,128)S(1)}) fusion(f32[1,2,32,128]{3,2,1,0:T(8,128)S(1)} %get-tuple-element.111, f32[1,2,32,128]{3,2,1,0:T(8,128)S(1)} %get-tuple-element.110, f32[1,2,32,128]{3,2,1,0:T(8,128)S(1)} %get-tuple-element.109, f32[]{:T(128)} %bitcast.29, f32[]{:T(128)} %bitcast.26, ...), kind=kLoop, calls=%fused_computation.378 | loop fusion | flops 81920 | bytes 163864 | tf_op jit(solution)/shard_map/add | solution.py:60
  104.3 5.2 %collective-permute-start.25 = (f32[3,1,256]{2,1,0:T(1,128)S(1)}, f32[3,1,256]{2,1,0:T(1,128)S(1)}, u32[]{:S(2)}, u32[]{:S(2)}) collective-permute-start(f32[3,1,256]{2,1,0:T(1,128)S(1)} %get-tuple-element.130), channel_id=1, source_target_pairs={{0,2},{2,4},{4,6},{6,8},{8,10},{10,12},{12,14},{14,16},{16,18},{18... | collective-permute-start | bytes 9224 | tf_op jit(solution)/shard_map/ppermute | solution.py:28
  110.8 5.4 %collective-permute-start.9 = (f32[3,4,1,128]{3,2,1,0:T(1,128)S(1)}, f32[3,4,1,128]{3,2,1,0:T(1,128)S(1)}, u32[]{:S(2)}, u32[]{:S(2)}) collective-permute-start(f32[3,4,1,128]{3,2,1,0:T(1,128)S(1)} %get-tuple-element.144), channel_id=1, source_target_pairs={{0,2},{2,4},{4,6},{1,3},{3,5},{5,7},{8,10},{10,12},{12,14},{9,11},... | collective-permute-start | bytes 18440 | tf_op jit(solution)/shard_map/ppermute | solution.py:28
  133.1 3.8 %multiply_add_fusion.51 = (f32[1,2,32,128]{3,2,1,0:T(8,128)S(1)}, f32[1,2,32,128]{3,2,1,0:T(8,128)S(1)}) fusion(f32[1,2,32,128]{3,2,1,0:T(8,128)S(1)} %get-tuple-element.93, f32[1,2,32,128]{3,2,1,0:T(8,128)S(1)} %get-tuple-element.92, f32[1,2,32,128]{3,2,1,0:T(8,128)S(1)} %get-tuple-element.91, f32[]{:T(128)} %bitcast.17, f32[]{:T(128)} %bitcast.16, ...), kind=kLoop, calls=%fused_computation.368 | loop fusion | flops 81920 | bytes 163864 | tf_op jit(solution)/shard_map/add | solution.py:49
  144.5 3.8 %multiply_add_fusion.45 = (f32[1,2,32,128]{3,2,1,0:T(8,128)S(1)}, f32[1,2,32,128]{3,2,1,0:T(8,128)S(1)}) fusion(f32[1,2,32,128]{3,2,1,0:T(8,128)S(1)} %get-tuple-element.85, f32[1,2,32,128]{3,2,1,0:T(8,128)S(1)} %get-tuple-element.84, f32[1,2,32,128]{3,2,1,0:T(8,128)S(1)} %get-tuple-element.83, f32[]{:T(128)} %bitcast.27, f32[]{:T(128)} %bitcast.26, ...), kind=kLoop, calls=%fused_computation.362 | loop fusion | flops 81920 | bytes 163864 | tf_op jit(solution)/shard_map/add | solution.py:49
  150.3 3.8 %multiply_add_fusion.42 = (f32[1,2,32,128]{3,2,1,0:T(8,128)S(1)}, f32[1,2,32,128]{3,2,1,0:T(8,128)S(1)}) fusion(f32[1,2,32,128]{3,2,1,0:T(8,128)S(1)} %get-tuple-element.81, f32[1,2,32,128]{3,2,1,0:T(8,128)S(1)} %get-tuple-element.80, f32[1,2,32,128]{3,2,1,0:T(8,128)S(1)} %get-tuple-element.79, f32[]{:T(128)} %bitcast.29, f32[]{:T(128)} %bitcast.26, ...), kind=kLoop, calls=%fused_computation.359 | loop fusion | flops 81920 | bytes 163864 | tf_op jit(solution)/shard_map/add | solution.py:60
  154.3 4.5 %collective-permute-start.13 = (f32[3,1,32,128]{3,2,1,0:T(8,128)S(1)}, f32[3,1,32,128]{3,2,1,0:T(8,128)S(1)}, u32[]{:S(2)}, u32[]{:S(2)}) collective-permute-start(f32[3,1,32,128]{3,2,1,0:T(8,128)S(1)} %get-tuple-element.190), channel_id=1, source_target_pairs={{0,8},{8,16},{16,24},{1,9},{9,17},{17,25},{2,10},{10,18},{18,26},{... | collective-permute-start | bytes 147464 | tf_op jit(solution)/shard_map/ppermute | solution.py:28
  160.6 4.3 %collective-permute-done.12 = f32[3,1,32,128]{3,2,1,0:T(8,128)S(1)} collective-permute-done((f32[3,1,32,128]{3,2,1,0:T(8,128)S(1)}, f32[3,1,32,128]{3,2,1,0:T(8,128)S(1)}, u32[]{:S(2)}, u32[]{:S(2)}) %collective-permute-start.12) | collective-permute-done | bytes 49184 | tf_op jit(solution)/shard_map/ppermute | solution.py:30
  166.2 5.4 %collective-permute-start.15 = (f32[3,4,1,128]{3,2,1,0:T(1,128)S(1)}, f32[3,4,1,128]{3,2,1,0:T(1,128)S(1)}, u32[]{:S(2)}, u32[]{:S(2)}) collective-permute-start(f32[3,4,1,128]{3,2,1,0:T(1,128)S(1)} %get-tuple-element.142), channel_id=1, source_target_pairs={{0,2},{2,4},{4,6},{1,3},{3,5},{5,7},{8,10},{10,12},{12,14},{9,11},... | collective-permute-start | bytes 18440 | tf_op jit(solution)/shard_map/ppermute | solution.py:28
  188.4 3.8 %multiply_add_fusion.33 = (f32[1,2,32,128]{3,2,1,0:T(8,128)S(1)}, f32[1,2,32,128]{3,2,1,0:T(8,128)S(1)}) fusion(f32[1,2,32,128]{3,2,1,0:T(8,128)S(1)} %get-tuple-element.63, f32[1,2,32,128]{3,2,1,0:T(8,128)S(1)} %get-tuple-element.62, f32[1,2,32,128]{3,2,1,0:T(8,128)S(1)} %get-tuple-element.61, f32[]{:T(128)} %bitcast.17, f32[]{:T(128)} %bitcast.16, ...), kind=kLoop, calls=%fused_computation.349 | loop fusion | flops 81920 | bytes 163864 | tf_op jit(solution)/shard_map/add | solution.py:49
  199.9 3.8 %multiply_add_fusion.27 = (f32[1,2,32,128]{3,2,1,0:T(8,128)S(1)}, f32[1,2,32,128]{3,2,1,0:T(8,128)S(1)}) fusion(f32[1,2,32,128]{3,2,1,0:T(8,128)S(1)} %get-tuple-element.55, f32[1,2,32,128]{3,2,1,0:T(8,128)S(1)} %get-tuple-element.54, f32[1,2,32,128]{3,2,1,0:T(8,128)S(1)} %get-tuple-element.53, f32[]{:T(128)} %bitcast.27, f32[]{:T(128)} %bitcast.26, ...), kind=kLoop, calls=%fused_computation.343 | loop fusion | flops 81920 | bytes 163864 | tf_op jit(solution)/shard_map/add | solution.py:49
  220.3 5.4 %collective-permute-start.21 = (f32[3,4,1,128]{3,2,1,0:T(1,128)S(1)}, f32[3,4,1,128]{3,2,1,0:T(1,128)S(1)}, u32[]{:S(2)}, u32[]{:S(2)}) collective-permute-start(f32[3,4,1,128]{3,2,1,0:T(1,128)S(1)} %get-tuple-element.140), channel_id=1, source_target_pairs={{0,2},{2,4},{4,6},{1,3},{3,5},{5,7},{8,10},{10,12},{12,14},{9,11},... | collective-permute-start | bytes 18440 | tf_op jit(solution)/shard_map/ppermute | solution.py:28
  242.5 3.8 %multiply_add_fusion.15 = (f32[1,2,32,128]{3,2,1,0:T(8,128)S(1)}, f32[1,2,32,128]{3,2,1,0:T(8,128)S(1)}) fusion(f32[1,2,32,128]{3,2,1,0:T(8,128)S(1)} %get-tuple-element.33, f32[1,2,32,128]{3,2,1,0:T(8,128)S(1)} %get-tuple-element.32, f32[1,2,32,128]{3,2,1,0:T(8,128)S(1)} %get-tuple-element.31, f32[]{:T(128)} %bitcast.17, f32[]{:T(128)} %bitcast.16, ...), kind=kLoop, calls=%fused_computation.330 | loop fusion | flops 81920 | bytes 163864 | tf_op jit(solution)/shard_map/add | solution.py:49
  254.0 3.8 %multiply_add_fusion.9 = (f32[1,2,32,128]{3,2,1,0:T(8,128)S(1)}, f32[1,2,32,128]{3,2,1,0:T(8,128)S(1)}) fusion(f32[1,2,32,128]{3,2,1,0:T(8,128)S(1)} %get-tuple-element.25, f32[1,2,32,128]{3,2,1,0:T(8,128)S(1)} %get-tuple-element.24, f32[1,2,32,128]{3,2,1,0:T(8,128)S(1)} %get-tuple-element.23, f32[]{:T(128)} %bitcast.27, f32[]{:T(128)} %bitcast.26, ...), kind=kLoop, calls=%fused_computation.324 | loop fusion | flops 81920 | bytes 163864 | tf_op jit(solution)/shard_map/add | solution.py:49
  259.8 3.8 %multiply_add_fusion.6 = (f32[1,2,32,128]{3,2,1,0:T(8,128)S(1)}, f32[1,2,32,128]{3,2,1,0:T(8,128)S(1)}) fusion(f32[1,2,32,128]{3,2,1,0:T(8,128)S(1)} %get-tuple-element.21, f32[1,2,32,128]{3,2,1,0:T(8,128)S(1)} %get-tuple-element.20, f32[1,2,32,128]{3,2,1,0:T(8,128)S(1)} %get-tuple-element.19, f32[]{:T(128)} %bitcast.29, f32[]{:T(128)} %bitcast.26, ...), kind=kLoop, calls=%fused_computation.321 | loop fusion | flops 81920 | bytes 163864 | tf_op jit(solution)/shard_map/add | solution.py:60
  264.6 10.6 %all-gather = f32[24,4,16]{2,1,0:T(4,128)S(1)} all-gather(f32[3,4,16]{2,1,0:T(4,128)S(1)} %broadcast_multiply_fusion), channel_id=2, replica_groups=mesh['region'=4,'gx'=4,'gy'=2] {'gx','gy'}, dimensions={0}, use_global_device_ids=true | all-gather | bytes 6912 | tf_op jit(solution)/shard_map/all_gather | solution.py:158
  278.1 4.5 %collective-permute-start.29 = (f32[3,1,256]{2,1,0:T(1,128)S(1)}, f32[3,1,256]{2,1,0:T(1,128)S(1)}, u32[]{:S(2)}, u32[]{:S(2)}) collective-permute-start(f32[3,1,256]{2,1,0:T(1,128)S(1)} %get-tuple-element.128), channel_id=1, source_target_pairs={{0,2},{2,4},{4,6},{6,8},{8,10},{10,12},{12,14},{14,16},{16,18},{18... | collective-permute-start | bytes 9224 | tf_op jit(solution)/shard_map/ppermute | solution.py:28
  (181 shorter events, 139.7 us)
Async XLA Ops:
  1.5 51.3 %collective-permute-start.1 = (f32[3,1,32,128]{3,2,1,0:T(8,128)S(1)}, f32[3,1,32,128]{3,2,1,0:T(8,128)S(1)}, u32[]{:S(2)}, u32[]{:S(2)}) collective-permute-start(f32[3,1,32,128]{3,2,1,0:T(8,128)S(1)} %get-tuple-element.224), channel_id=1, source_target_pairs={{0,8},{8,16},{16,24},{1,9},{9,17},{17,25},{2,10},{10,18},{18,26},{... | collective-permute-start | bytes 147464 | tf_op jit(solution)/shard_map/ppermute | solution.py:28
  6.4 47.4 %collective-permute-start = (f32[3,1,32,128]{3,2,1,0:T(8,128)S(1)}, f32[3,1,32,128]{3,2,1,0:T(8,128)S(1)}, u32[]{:S(2)}, u32[]{:S(2)}) collective-permute-start(f32[3,1,32,128]{3,2,1,0:T(8,128)S(1)} %get-tuple-element.225), channel_id=1, source_target_pairs={{8,0},{16,8},{24,16},{9,1},{17,9},{25,17},{10,2},{18,10},{26,18},{... | collective-permute-start | bytes 147464 | tf_op jit(solution)/shard_map/ppermute | solution.py:30
  53.8 16.5 %collective-permute-start.3 = (f32[3,4,1,128]{3,2,1,0:T(1,128)S(1)}, f32[3,4,1,128]{3,2,1,0:T(1,128)S(1)}, u32[]{:S(2)}, u32[]{:S(2)}) collective-permute-start(f32[3,4,1,128]{3,2,1,0:T(1,128)S(1)} %get-tuple-element.150), channel_id=1, source_target_pairs={{0,2},{2,4},{4,6},{1,3},{3,5},{5,7},{8,10},{10,12},{12,14},{9,11},... | collective-permute-start | bytes 18440 | tf_op jit(solution)/shard_map/ppermute | solution.py:28
  58.0 12.3 %collective-permute-start.2 = (f32[3,4,1,128]{3,2,1,0:T(1,128)S(1)}, f32[3,4,1,128]{3,2,1,0:T(1,128)S(1)}, u32[]{:S(2)}, u32[]{:S(2)}) collective-permute-start(f32[3,4,1,128]{3,2,1,0:T(1,128)S(1)} %get-tuple-element.151), channel_id=1, source_target_pairs={{2,0},{4,2},{6,4},{3,1},{5,3},{7,5},{10,8},{12,10},{14,12},{11,9},... | collective-permute-start | bytes 18440 | tf_op jit(solution)/shard_map/ppermute | solution.py:30
  70.5 15.0 %collective-permute-start.4 = (f32[3,4,34,1]{3,2,1,0:T(8,128)S(1)}, f32[3,4,34,1]{3,2,1,0:T(8,128)S(1)}, u32[]{:S(2)}, u32[]{:S(2)}) collective-permute-start(f32[3,4,34,1]{3,2,1,0:T(8,128)S(1)} %get-tuple-element.139), channel_id=1, source_target_pairs={{1,0},{3,2},{5,4},{7,6},{9,8},{11,10},{13,12},{15,14},{17,16},{19,... | collective-permute-start | bytes 4904 | tf_op jit(solution)/shard_map/ppermute | solution.py:30
  71.8 19.5 %collective-permute-start.5 = (f32[3,4,34,1]{3,2,1,0:T(8,128)S(1)}, f32[3,4,34,1]{3,2,1,0:T(8,128)S(1)}, u32[]{:S(2)}, u32[]{:S(2)}) collective-permute-start(f32[3,4,34,1]{3,2,1,0:T(8,128)S(1)} %get-tuple-element.138), channel_id=1, source_target_pairs={{0,1},{2,3},{4,5},{6,7},{8,9},{10,11},{12,13},{14,15},{16,17},{18,... | collective-permute-start | bytes 4904 | tf_op jit(solution)/shard_map/ppermute | solution.py:28
  98.1 11.4 %collective-permute-start.7 = (f32[3,1,32,128]{3,2,1,0:T(8,128)S(1)}, f32[3,1,32,128]{3,2,1,0:T(8,128)S(1)}, u32[]{:S(2)}, u32[]{:S(2)}) collective-permute-start(f32[3,1,32,128]{3,2,1,0:T(8,128)S(1)} %get-tuple-element.208), channel_id=1, source_target_pairs={{0,8},{8,16},{16,24},{1,9},{9,17},{17,25},{2,10},{10,18},{18,26},{... | collective-permute-start | bytes 147464 | tf_op jit(solution)/shard_map/ppermute | solution.py:28
  101.6 7.9 %collective-permute-start.6 = (f32[3,1,32,128]{3,2,1,0:T(8,128)S(1)}, f32[3,1,32,128]{3,2,1,0:T(8,128)S(1)}, u32[]{:S(2)}, u32[]{:S(2)}) collective-permute-start(f32[3,1,32,128]{3,2,1,0:T(8,128)S(1)} %get-tuple-element.209), channel_id=1, source_target_pairs={{8,0},{16,8},{24,16},{9,1},{17,9},{25,17},{10,2},{18,10},{26,18},{... | collective-permute-start | bytes 147464 | tf_op jit(solution)/shard_map/ppermute | solution.py:30
  103.0 57.2 %collective-permute-start.24 = (f32[3,1,256]{2,1,0:T(1,128)S(1)}, f32[3,1,256]{2,1,0:T(1,128)S(1)}, u32[]{:S(2)}, u32[]{:S(2)}) collective-permute-start(f32[3,1,256]{2,1,0:T(1,128)S(1)} %get-tuple-element.131), channel_id=1, source_target_pairs={{2,0},{4,2},{6,4},{8,6},{10,8},{12,10},{14,12},{16,14},{18,16},{20... | collective-permute-start | bytes 9224 | tf_op jit(solution)/shard_map/ppermute | solution.py:30
  104.3 55.9 %collective-permute-start.25 = (f32[3,1,256]{2,1,0:T(1,128)S(1)}, f32[3,1,256]{2,1,0:T(1,128)S(1)}, u32[]{:S(2)}, u32[]{:S(2)}) collective-permute-start(f32[3,1,256]{2,1,0:T(1,128)S(1)} %get-tuple-element.130), channel_id=1, source_target_pairs={{0,2},{2,4},{4,6},{6,8},{8,10},{10,12},{12,14},{14,16},{16,18},{18... | collective-permute-start | bytes 9224 | tf_op jit(solution)/shard_map/ppermute | solution.py:28
  109.5 17.1 %collective-permute-start.8 = (f32[3,4,1,128]{3,2,1,0:T(1,128)S(1)}, f32[3,4,1,128]{3,2,1,0:T(1,128)S(1)}, u32[]{:S(2)}, u32[]{:S(2)}) collective-permute-start(f32[3,4,1,128]{3,2,1,0:T(1,128)S(1)} %get-tuple-element.145), channel_id=1, source_target_pairs={{2,0},{4,2},{6,4},{3,1},{5,3},{7,5},{10,8},{12,10},{14,12},{11,9},... | collective-permute-start | bytes 18440 | tf_op jit(solution)/shard_map/ppermute | solution.py:30
  110.8 15.8 %collective-permute-start.9 = (f32[3,4,1,128]{3,2,1,0:T(1,128)S(1)}, f32[3,4,1,128]{3,2,1,0:T(1,128)S(1)}, u32[]{:S(2)}, u32[]{:S(2)}) collective-permute-start(f32[3,4,1,128]{3,2,1,0:T(1,128)S(1)} %get-tuple-element.144), channel_id=1, source_target_pairs={{0,2},{2,4},{4,6},{1,3},{3,5},{5,7},{8,10},{10,12},{12,14},{9,11},... | collective-permute-start | bytes 18440 | tf_op jit(solution)/shard_map/ppermute | solution.py:28
  126.8 15.7 %collective-permute-start.10 = (f32[3,4,34,1]{3,2,1,0:T(8,128)S(1)}, f32[3,4,34,1]{3,2,1,0:T(8,128)S(1)}, u32[]{:S(2)}, u32[]{:S(2)}) collective-permute-start(f32[3,4,34,1]{3,2,1,0:T(8,128)S(1)} %get-tuple-element.137), channel_id=1, source_target_pairs={{1,0},{3,2},{5,4},{7,6},{9,8},{11,10},{13,12},{15,14},{17,16},{19,... | collective-permute-start | bytes 4904 | tf_op jit(solution)/shard_map/ppermute | solution.py:30
  128.1 20.2 %collective-permute-start.11 = (f32[3,4,34,1]{3,2,1,0:T(8,128)S(1)}, f32[3,4,34,1]{3,2,1,0:T(8,128)S(1)}, u32[]{:S(2)}, u32[]{:S(2)}) collective-permute-start(f32[3,4,34,1]{3,2,1,0:T(8,128)S(1)} %get-tuple-element.136), channel_id=1, source_target_pairs={{0,1},{2,3},{4,5},{6,7},{8,9},{10,11},{12,13},{14,15},{16,17},{18,... | collective-permute-start | bytes 4904 | tf_op jit(solution)/shard_map/ppermute | solution.py:28
  164.9 17.1 %collective-permute-start.14 = (f32[3,4,1,128]{3,2,1,0:T(1,128)S(1)}, f32[3,4,1,128]{3,2,1,0:T(1,128)S(1)}, u32[]{:S(2)}, u32[]{:S(2)}) collective-permute-start(f32[3,4,1,128]{3,2,1,0:T(1,128)S(1)} %get-tuple-element.143), channel_id=1, source_target_pairs={{2,0},{4,2},{6,4},{3,1},{5,3},{7,5},{10,8},{12,10},{14,12},{11,9},... | collective-permute-start | bytes 18440 | tf_op jit(solution)/shard_map/ppermute | solution.py:30
  166.2 15.8 %collective-permute-start.15 = (f32[3,4,1,128]{3,2,1,0:T(1,128)S(1)}, f32[3,4,1,128]{3,2,1,0:T(1,128)S(1)}, u32[]{:S(2)}, u32[]{:S(2)}) collective-permute-start(f32[3,4,1,128]{3,2,1,0:T(1,128)S(1)} %get-tuple-element.142), channel_id=1, source_target_pairs={{0,2},{2,4},{4,6},{1,3},{3,5},{5,7},{8,10},{10,12},{12,14},{9,11},... | collective-permute-start | bytes 18440 | tf_op jit(solution)/shard_map/ppermute | solution.py:28
  182.2 15.7 %collective-permute-start.16 = (f32[3,4,34,1]{3,2,1,0:T(8,128)S(1)}, f32[3,4,34,1]{3,2,1,0:T(8,128)S(1)}, u32[]{:S(2)}, u32[]{:S(2)}) collective-permute-start(f32[3,4,34,1]{3,2,1,0:T(8,128)S(1)} %get-tuple-element.135), channel_id=1, source_target_pairs={{1,0},{3,2},{5,4},{7,6},{9,8},{11,10},{13,12},{15,14},{17,16},{19,... | collective-permute-start | bytes 4904 | tf_op jit(solution)/shard_map/ppermute | solution.py:30
  183.5 20.2 %collective-permute-start.17 = (f32[3,4,34,1]{3,2,1,0:T(8,128)S(1)}, f32[3,4,34,1]{3,2,1,0:T(8,128)S(1)}, u32[]{:S(2)}, u32[]{:S(2)}) collective-permute-start(f32[3,4,34,1]{3,2,1,0:T(8,128)S(1)} %get-tuple-element.134), channel_id=1, source_target_pairs={{0,1},{2,3},{4,5},{6,7},{8,9},{10,11},{12,13},{14,15},{16,17},{18,... | collective-permute-start | bytes 4904 | tf_op jit(solution)/shard_map/ppermute | solution.py:28
  214.4 60.8 %collective-permute-start.27 = (f32[3,130,1]{2,1,0:T(8,128)S(1)}, f32[3,130,1]{2,1,0:T(8,128)S(1)}, u32[]{:S(2)}, u32[]{:S(2)}) collective-permute-start(f32[3,130,1]{2,1,0:T(8,128)S(1)} %get-tuple-element.127), channel_id=1, source_target_pairs={{0,1},{2,3},{4,5},{6,7},{8,9},{10,11},{12,13},{14,15},{16,17},{18,... | collective-permute-start | bytes 4688 | tf_op jit(solution)/shard_map/ppermute | solution.py:28
  215.7 59.5 %collective-permute-start.26 = (f32[3,130,1]{2,1,0:T(8,128)S(1)}, f32[3,130,1]{2,1,0:T(8,128)S(1)}, u32[]{:S(2)}, u32[]{:S(2)}) collective-permute-start(f32[3,130,1]{2,1,0:T(8,128)S(1)} %get-tuple-element.126), channel_id=1, source_target_pairs={{1,0},{3,2},{5,4},{7,6},{9,8},{11,10},{13,12},{15,14},{17,16},{19,... | collective-permute-start | bytes 4688 | tf_op jit(solution)/shard_map/ppermute | solution.py:30
  219.0 17.1 %collective-permute-start.20 = (f32[3,4,1,128]{3,2,1,0:T(1,128)S(1)}, f32[3,4,1,128]{3,2,1,0:T(1,128)S(1)}, u32[]{:S(2)}, u32[]{:S(2)}) collective-permute-start(f32[3,4,1,128]{3,2,1,0:T(1,128)S(1)} %get-tuple-element.141), channel_id=1, source_target_pairs={{2,0},{4,2},{6,4},{3,1},{5,3},{7,5},{10,8},{12,10},{14,12},{11,9},... | collective-permute-start | bytes 18440 | tf_op jit(solution)/shard_map/ppermute | solution.py:30
  220.3 15.8 %collective-permute-start.21 = (f32[3,4,1,128]{3,2,1,0:T(1,128)S(1)}, f32[3,4,1,128]{3,2,1,0:T(1,128)S(1)}, u32[]{:S(2)}, u32[]{:S(2)}) collective-permute-start(f32[3,4,1,128]{3,2,1,0:T(1,128)S(1)} %get-tuple-element.140), channel_id=1, source_target_pairs={{0,2},{2,4},{4,6},{1,3},{3,5},{5,7},{8,10},{10,12},{12,14},{9,11},... | collective-permute-start | bytes 18440 | tf_op jit(solution)/shard_map/ppermute | solution.py:28
  236.3 15.7 %collective-permute-start.22 = (f32[3,4,34,1]{3,2,1,0:T(8,128)S(1)}, f32[3,4,34,1]{3,2,1,0:T(8,128)S(1)}, u32[]{:S(2)}, u32[]{:S(2)}) collective-permute-start(f32[3,4,34,1]{3,2,1,0:T(8,128)S(1)} %get-tuple-element.133), channel_id=1, source_target_pairs={{1,0},{3,2},{5,4},{7,6},{9,8},{11,10},{13,12},{15,14},{17,16},{19,... | collective-permute-start | bytes 4904 | tf_op jit(solution)/shard_map/ppermute | solution.py:30
  237.6 20.2 %collective-permute-start.23 = (f32[3,4,34,1]{3,2,1,0:T(8,128)S(1)}, f32[3,4,34,1]{3,2,1,0:T(8,128)S(1)}, u32[]{:S(2)}, u32[]{:S(2)}) collective-permute-start(f32[3,4,34,1]{3,2,1,0:T(8,128)S(1)} %get-tuple-element.132), channel_id=1, source_target_pairs={{0,1},{2,3},{4,5},{6,7},{8,9},{10,11},{12,13},{14,15},{16,17},{18,... | collective-permute-start | bytes 4904 | tf_op jit(solution)/shard_map/ppermute | solution.py:28
  (15 other events, 53.2 us)
where the time goes:
time: 296 us; the launch traced here: 290 us
  other arithmetic  137 us (46%)
  starting transfers between devices  82.1 us (28%)
  blocking collectives  52.3 us (18%)
  waiting for transfers between devices  9.92 us (3%)
  local copies, waits for them, and re-layouts  7.34 us (2%)
    add x23, other arithmetic, apply_transposed(): matrix[0, component] * vector[0] + matrix[1, component] * vector[1]  72.3 us
    ppermute x16, starting transfers between devices, extended(): lax.ppermute(tail, axis, [(i, (i + 1) % count) for i in range(ends)])  61.4 us
    add x19, other arithmetic, apply_kernel(): matrix[component, 0] * vector[0] + matrix[component, 1] * vector[1]  60.2 us
    psum x1, blocking collectives, spread(): return lax.psum(kept, axis)  41.8 us
    ppermute x16, starting transfers between devices, extended(): lax.ppermute(head, axis, [((i + 1) % count, i) for i in range(ends)])  20.7 us
    all_gather x1, blocking collectives, body(): gathered = lax.all_gather(averages[None], ('gx', 'gy'), axis=0, tiled=True)  10.6 us
    ppermute x16, waiting for transfers between devices, extended(): lax.ppermute(head, axis, [((i + 1) % count, i) for i in range(ends)])  8.25 us
  transfers between devices with their start and end apart: 32, of which 5 were waited for; matrix products, arithmetic and copies ran while one was open for 43% of the time, Pallas kernels for 0%

commit v1 on v0

--- a/solution.py
+++ b/solution.py
@@ -1,6 +1,10 @@
+import functools
+
 import jax
 import jax.numpy as jnp
 from jax import lax
+from jax.experimental import pallas as pl
+from jax.experimental.pallas import tpu as pltpu
 from jax.sharding import PartitionSpec as P
 
 K = 8
@@ -118,7 +122,7 @@
     return extended(magnet, ((("region", "gx"), 1), ("gy", 2)), 1)
 
 
-def body(spins, uniforms, trials, exch_kernel, film_m, film_anis):
+def body_general(spins, uniforms, trials, exch_kernel, film_m, film_anis):
     layers_dev = spins.shape[1]
     rows_x = spins.shape[2]
     rows_y = spins.shape[3]
@@ -177,6 +181,569 @@
     return (stack_spins, normalized(corrected))
 
 
+LANES = 128
+EDGE = 8
+ROUNDS = 2 * SWEEPS
+MESH = pl.DeviceIdType.MESH
+
+
+def kernel_fits(spins, film_m, counts):
+    _, gx_count, gy_count = counts
+    _, _, rows_x, rows_y = spins.shape
+    cells_x, cells_y = rows_x // K * gx_count, rows_y // K * gy_count
+    return (
+        rows_y == LANES
+        and rows_x % 16 == 0
+        and EDGE % (rows_x // K) == 0
+        and cells_x % EDGE == 0
+        and 3 * cells_y <= LANES
+        and 3 * (rows_x // K) <= 16
+        and film_m.shape[1] % 16 == 0
+        and cells_x + 16 <= film_m.shape[1]
+        and film_m.shape[2] % LANES == 0
+        and cells_y + 2 <= film_m.shape[2]
+        and 3 * spins.shape[1] <= EDGE
+    )
+
+
+def unit(vector):
+    scale = lax.rsqrt(vector[0] * vector[0] + vector[1] * vector[1] + vector[2] * vector[2])
+    return [part * scale for part in vector]
+
+
+def cross(left, right):
+    return [
+        left[1] * right[2] - left[2] * right[1],
+        left[2] * right[0] - left[0] * right[2],
+        left[0] * right[1] - left[1] * right[0],
+    ]
+
+
+def fused_kernel(
+    counts,
+    exch,
+    spins_hbm,
+    unif_hbm,
+    trial_hbm,
+    film_hbm,
+    anis_hbm,
+    spins_out,
+    film_out,
+    stack,
+    unif,
+    trial,
+    film_near,
+    film,
+    trial_film,
+    half_film,
+    anis,
+    x_send,
+    x_recv,
+    y_send,
+    y_recv,
+    z_recv,
+    fx_send,
+    fx_recv,
+    fy_send,
+    fy_recv,
+    cell_all,
+    cell_own,
+    mean_send,
+    mean_recv,
+    inter,
+    local_sem,
+    send_sem,
+    recv_sem,
+    film_send_sem,
+    film_recv_sem,
+    cell_send_sem,
+    cell_recv_sem,
+    mean_send_sem,
+    mean_recv_sem,
+):
+    regions, gx_count, gy_count = counts
+    layers, rows = spins_hbm.shape[1], spins_hbm.shape[2]
+    film_rows, film_cols = film_hbm.shape[1], film_hbm.shape[2]
+    piece_x, piece_y = rows // K, LANES // K
+    cells_x, cells_y = piece_x * gx_count, piece_y * gy_count
+    per_tile = EDGE // piece_x
+    inner = pl.ds(EDGE, rows)
+    film_inner = pl.ds(EDGE, film_rows)
+    region = lax.axis_index("region")
+    gx = lax.axis_index("gx")
+    gy = lax.axis_index("gy")
+    first = (region == 0) & (gx == 0) & (gy == 0)
+    not_first = jnp.logical_not(first)
+
+    places = [
+        (region > 0, (region - 1, gx, gy)),
+        (region < regions - 1, (region + 1, gx, gy)),
+        (gx > 0, (region, gx - 1, gy)),
+        (gx < gx_count - 1, (region, gx + 1, gy)),
+        (gy > 0, (region, gx, gy - 1)),
+        (gy < gy_count - 1, (region, gx, gy + 1)),
+    ]
+    line = region * gx_count + gx
+    film_places = [
+        (line > 0, ((line + gx_count * regions - 1) // gx_count % regions, (gx + gx_count - 1) % gx_count, gy)),
+        (line < regions * gx_count - 1, ((line + 1) // gx_count % regions, (gx + 1) % gx_count, gy)),
+        places[4],
+        places[5],
+    ]
+
+    loads = [
+        pltpu.make_async_copy(source, target, local_sem.at[at])
+        for at, (source, target) in enumerate(
+            [
+                (spins_hbm, stack.at[0, :, :, inner, :]),
+                (film_hbm, film.at[:, film_inner, :]),
+                (trial_hbm, trial),
+                (unif_hbm, unif),
+                (anis_hbm, anis),
+            ]
+        )
+    ]
+    for load in loads:
+        load.start()
+
+    barrier = pltpu.get_barrier_semaphore()
+    for there, place in places + film_places[:2]:
+
+        @pl.when(there)
+        def _(place=place):
+            pl.semaphore_signal(barrier, inc=1, device_id=place, device_id_type=MESH)
+
+    @pl.when(not_first)
+    def _():
+        pl.semaphore_signal(barrier, inc=1, device_id=(0, 0, 0), device_id_type=MESH)
+
+    @pl.when(first)
+    def _():
+        for gx_at in range(gx_count):
+            for gy_at in range(gy_count):
+                if gx_at or gy_at:
+                    pl.semaphore_signal(barrier, inc=1, device_id=(0, gx_at, gy_at), device_id_type=MESH)
+
+    lane = lax.broadcasted_iota(jnp.int32, (rows, LANES), 1)
+    film_lane = lax.broadcasted_iota(jnp.int32, (film_rows, LANES), 1)
+
+    def halo(turn, way):
+        if way < 2:
+            source = stack.at[turn, :, 0 if way == 0 else layers - 1, inner, :]
+            return source, z_recv
+        if way < 4:
+            return x_send.at[turn, way - 2], x_recv
+        return y_send.at[turn, way - 4], y_recv
+
+    def halo_copy(turn, way, slot):
+        source, target = halo(turn, way)
+        return pltpu.make_async_remote_copy(
+            src_ref=source,
+            dst_ref=target.at[turn, slot % 2],
+            send_sem=send_sem.at[turn, way],
+            recv_sem=recv_sem.at[turn, slot],
+            device_id=places[way][1],
+            device_id_type=MESH,
+        )
+
+    def film_copy(turn, way, slot):
+        source, target = (fx_send, fx_recv) if way < 2 else (fy_send, fy_recv)
+        return pltpu.make_async_remote_copy(
+            src_ref=source.at[turn, way % 2],
+            dst_ref=target.at[turn, slot % 2],
+            send_sem=film_send_sem.at[turn, way],
+            recv_sem=film_recv_sem.at[turn, slot],
+            device_id=film_places[way][1],
+            device_id_type=MESH,
+        )
+
+    def pack_halo(turn):
+        right = jnp.zeros((rows, LANES), jnp.float32)
+        left = right
+        for part in range(3):
+            for layer in range(layers):
+                at = part * layers + layer
+                block = stack[turn, part, layer, inner, :]
+                x_send[turn, 0, at : at + 1, :] = stack[turn, part, layer, EDGE : EDGE + 1, :]
+                x_send[turn, 1, at : at + 1, :] = stack[turn, part, layer, EDGE + rows - 1 : EDGE + rows, :]
+                left = jnp.where(lane == at, pltpu.roll(block, at, 1) if at else block, left)
+                right = jnp.where(lane == at, pltpu.roll(block, at + 1, 1), right)
+        y_send[turn, 0] = left
+        y_send[turn, 1] = right
+
+    def send_halo(turn, ways):
+        for way in ways:
+
+            @pl.when(places[way][0])
+            def _(way=way):
+                halo_copy(turn, way, way ^ 1).start()
+
+    def take_halo(turn):
+        for way in range(6):
+
+            @pl.when(places[way][0])
+            def _(way=way):
+                halo_copy(turn, way, way).wait_recv()
+
+        for part in range(3):
+            for layer in range(layers):
+                at = part * layers + layer
+                stack[turn, part, layer, EDGE - 1 : EDGE, :] = x_recv[turn, 0, at : at + 1, :]
+                stack[turn, part, layer, EDGE + rows : EDGE + rows + 1, :] = x_recv[turn, 1, at : at + 1, :]
+
+    def pack_film(turn, source):
+        left = jnp.zeros((film_rows, LANES), jnp.float32)
+        right = left
+        for part in range(3):
+            fx_send[turn, 0, part : part + 1, :] = source[part, EDGE : EDGE + 1, :]
+            fx_send[turn, 1, part : part + 1, :] = source[part, EDGE + film_rows - 1 : EDGE + film_rows, :]
+            head = source[part, film_inner, :LANES]
+            tail = source[part, film_inner, film_cols - LANES :]
+            left = jnp.where(film_lane == part, pltpu.roll(head, part, 1) if part else head, left)
+            right = jnp.where(film_lane == part, pltpu.roll(tail, part + 1, 1), right)
+        fy_send[turn, 0] = left
+        fy_send[turn, 1] = right
+
+    def send_film(turn):
+        for way in range(4):
+
+            @pl.when(film_places[way][0])
+            def _(way=way):
+                film_copy(turn, way, way ^ 1).start()
+
+    def take_film(turn, target):
+        for way in range(4):
+
+            @pl.when(film_places[way][0])
+            def _(way=way):
+                film_copy(turn, way, way).wait_recv()
+
+        for part in range(3):
+            target[part, EDGE - 1 : EDGE, :] = fx_recv[turn, 0, part : part + 1, :]
+            target[part, EDGE + film_rows : EDGE + film_rows + 1, :] = fx_recv[turn, 1, part : part + 1, :]
+
+    def rate(turn, source, low, count, with_inter):
+        wide = lax.broadcasted_iota(jnp.int32, (count, film_cols), 1)
+        repeat = film_cols // LANES
+        magnet, field = [], []
+        for part in range(3):
+            at = EDGE + low
+            block = source[part, at : at + count, :]
+            before = pltpu.roll(fy_recv[turn, 0, low : low + count, :], (LANES - part) % LANES, 1) if part else fy_recv[turn, 0, low : low + count, :]
+            after = pltpu.roll(fy_recv[turn, 1, low : low + count, :], LANES - 1 - part, 1)
+            total = source[part, at - 1 : at - 1 + count, :] + source[part, at + 1 : at + 1 + count, :]
+            total = total + jnp.where(wide == 0, jnp.concatenate([before] * repeat, 1), pltpu.roll(block, 1, 1))
+            total = total + jnp.where(
+                wide == film_cols - 1, jnp.concatenate([after] * repeat, 1), pltpu.roll(block, film_cols - 1, 1)
+            )
+            total = total - 4.0 * block
+            if with_inter:
+                extra = coupling_up * inter[part, low : low + count, :]
+                rest = [jnp.zeros((count, LANES), jnp.float32)] * (repeat - 1)
+                total = total + jnp.concatenate([extra] + rest, 1)
+            magnet.append(block)
+            field.append(total)
+        field[2] = field[2] + anis[low : low + count, :] * magnet[2]
+        precession = cross(magnet, field)
+        relaxation = cross(magnet, precession)
+        factor = -1.0 / (1.0 + damping * damping)
+        return magnet, [factor * (one + damping * two) for one, two in zip(precession, relaxation)]
+
+    def film_start(low, count, with_inter=False):
+        magnet, speed = rate(0, film, low, count, with_inter)
+        for part in range(3):
+            trial_film[part, EDGE + low : EDGE + low + count, :] = magnet[part] + time_step * speed[part]
+            half_film[part, low : low + count, :] = magnet[part] + (0.5 * time_step) * speed[part]
+
+    def film_end(low, count, with_inter=False):
+        _, speed = rate(1, trial_film, low, count, with_inter)
+        result = unit([half_film[part, low : low + count, :] + (0.5 * time_step) * speed[part] for part in range(3)])
+        for part in range(3):
+            film_out[part, low : low + count, :] = result[part]
+
+    x_iota = lax.broadcasted_iota(jnp.int32, (rows, LANES), 0)
+
+    def half_sweep(turn):
+        sweep, colour = turn // 2, turn % 2
+        for layer in range(layers):
+            own = [stack[turn, part, layer, inner, :] for part in range(3)]
+            proposal = unit([own[part] + step_cone * trial[sweep, part, layer] for part in range(3)])
+            around = [[] for _ in range(6)]
+            for part in range(3):
+                at = part * layers + layer
+                around[0].append(z_recv[turn, 0, part] if layer == 0 else stack[turn, part, layer - 1, inner, :])
+                around[1].append(z_recv[turn, 1, part] if layer == layers - 1 else stack[turn, part, layer + 1, inner, :])
+                around[2].append(stack[turn, part, layer, EDGE - 1 : EDGE - 1 + rows, :])
+                around[3].append(stack[turn, part, layer, EDGE + 1 : EDGE + 1 + rows, :])
+                before = pltpu.roll(y_recv[turn, 0], LANES - at, 1) if at else y_recv[turn, 0]
+                after = pltpu.roll(y_recv[turn, 1], LANES - 1 - at, 1)
+                around[4].append(jnp.where(lane == 0, before, pltpu.roll(own[part], 1, 1)))
+                around[5].append(jnp.where(lane == LANES - 1, after, pltpu.roll(own[part], LANES - 1, 1)))
+            gain = jnp.zeros((rows, LANES), jnp.float32)
+            shift = [proposal[part] - own[part] for part in range(3)]
+            for part in range(3):
+                field = coupling_down * film_near[part]
+                for way in range(3):
+                    for other in range(3):
+                        field = field + exch[9 * way + 3 * part + other] * around[2 * way + 1][other]
+                        field = field + exch[9 * way + 3 * other + part] * around[2 * way][other]
+                gain = gain + shift[part] * field
+            change = -gain - anisotropy * (proposal[2] * proposal[2] - own[2] * own[2])
+            accept = jnp.exp(jnp.minimum(-inverse_temp * change, 0.0))
+            weight = 1.0 / (1.0 + jnp.exp((unif[sweep, layer] - accept) * (1.0 / softness)))
+            blended = unit([own[part] + weight * shift[part] for part in range(3)])
+            parity = (region * layers + layer + gx * rows + gy * LANES + x_iota + lane) % 2
+            for part in range(3):
+                fresh = jnp.where(parity == colour, blended[part], own[part])
+                if turn == ROUNDS - 1:
+                    spins_out[part, layer] = fresh
+                else:
+                    stack[turn + 1, part, layer, inner, :] = fresh
+
+    def cell_copy(region_at, gx_at, gy_at):
+        number = (region_at * gx_count + gx_at) * gy_count + gy_at
+        return pltpu.make_async_remote_copy(
+            src_ref=cell_all.at[pl.ds(gx_at // per_tile * EDGE, EDGE), :],
+            dst_ref=cell_own,
+            send_sem=cell_send_sem.at[number],
+            recv_sem=cell_recv_sem,
+            device_id=(region_at, gx_at, gy_at),
+            device_id_type=MESH,
+        )
+
+    others = [
+        (region_at, gx_at, gy_at)
+        for region_at in reversed(range(regions))
+        for gx_at in reversed(range(gx_count))
+        for gy_at in reversed(range(gy_count))
+        if region_at or gx_at or gy_at
+    ]
+
+    def mean_copy(gx_at, gy_at):
+        number = gx_at * gy_count + gy_at
+        return pltpu.make_async_remote_copy(
+            src_ref=mean_send,
+            dst_ref=mean_recv.at[number],
+            send_sem=mean_send_sem,
+            recv_sem=mean_recv_sem.at[number],
+            device_id=(0, 0, 0),
+            device_id_type=MESH,
+        )
+
+    for way in range(6):
+
+        @pl.when(jnp.logical_not(places[way][0]))
+        def _(way=way):
+            for turn in range(ROUNDS):
+                target = halo(turn, way)[1]
+                target[turn, way % 2] = jnp.zeros(target.shape[2:], jnp.float32)
+
+    for way in range(4):
+
+        @pl.when(jnp.logical_not(film_places[way][0]))
+        def _(way=way):
+            target = fx_recv if way < 2 else fy_recv
+            for turn in range(2):
+                target[turn, way % 2] = jnp.zeros(target.shape[2:], jnp.float32)
+
+    loads[0].wait()
+    pack_halo(0)
+    loads[1].wait()
+
+    @pl.when(first)
+    def _():
+        cell_lane = lax.broadcasted_iota(jnp.int32, (cells_x, LANES), 1)
+        packed = film[0, EDGE : EDGE + cells_x, :LANES]
+        for part in (1, 2):
+            moved = pltpu.roll(film[part, EDGE : EDGE + cells_x, :LANES], part * cells_y, 1)
+            packed = jnp.where(cell_lane >= part * cells_y, moved, packed)
+        cell_all[...] = packed
+        cell_own[...] = packed[:EDGE]
+
+    pack_film(0, film)
+
+    expected = sum(there.astype(jnp.int32) for there, _ in places + film_places[:2])
+    expected = expected + jnp.where(
+        first, regions * gx_count * gy_count - 1, jnp.where(region == 0, 1, 0)
+    )
+    pl.semaphore_wait(barrier, expected)
+
+    @pl.when(first)
+    def _():
+        for other in others:
+            cell_copy(*other).start()
+
+    send_halo(0, range(6))
+    send_film(0)
+    for load in loads[2:]:
+        load.wait()
+
+    @pl.when(not_first)
+    def _():
+        cell_copy(0, 0, 0).wait_recv()
+
+    row_at = lax.broadcasted_iota(jnp.int32, (LANES, LANES), 0)
+    col_at = lax.broadcasted_iota(jnp.int32, (LANES, LANES), 1)
+    pick_row = lax.broadcasted_iota(jnp.int32, (rows, EDGE), 0) // K + gx % per_tile * piece_x
+    pick = (lax.broadcasted_iota(jnp.int32, (rows, EDGE), 1) == pick_row).astype(jnp.float32)
+    dot = functools.partial(jnp.dot, precision=lax.Precision.HIGHEST, preferred_element_type=jnp.float32)
+    cells = jnp.where(
+        lax.broadcasted_iota(jnp.int32, (EDGE, LANES), 1) < 3 * cells_y, cell_own[...], 0.0
+    )
+    tall = dot(pick, cells)
+    for part in range(3):
+        spread_cols = (row_at == part * cells_y + gy * piece_y + col_at // K).astype(jnp.float32)
+        film_near[part] = dot(tall, spread_cols)
+
+    film_steps = list(range(0, film_rows, 16))
+    for turn in range(ROUNDS):
+        take_halo(turn)
+        half_sweep(turn)
+        if turn + 1 < ROUNDS:
+            pack_halo(turn + 1)
+            send_halo(turn + 1, range(6))
+        if turn == 0:
+            take_film(0, film)
+            for low in film_steps:
+                film_start(low, 16)
+            pack_film(1, trial_film)
+            send_film(1)
+        if turn == 1:
+            take_film(1, trial_film)
+            for low in film_steps[: len(film_steps) // 2]:
+                film_end(low, 16)
+        if turn == 2:
+            for low in film_steps[len(film_steps) // 2 :]:
+                film_end(low, 16)
+
+    @pl.when(region == 0)
+    def _():
+        for part in range(3):
+            for at in range(piece_x):
+                block = spins_out[part, 0, at * K : (at + 1) * K, :]
+                mean_send[part * piece_x + at : part * piece_x + at + 1, :] = jnp.sum(block, axis=0, keepdims=True)
+        for at in range(3 * piece_x, 16):
+            mean_send[at : at + 1, :] = jnp.zeros((1, LANES), jnp.float32)
+        gather_cols = jnp.where(col_at == row_at // K + gy * piece_y, 1.0 / (K * K), 0.0)
+        mean_send[...] = dot(mean_send[...], gather_cols)
+
+        @pl.when(not_first)
+        def _():
+            number = gx * gy_count + gy
+            pltpu.make_async_remote_copy(
+                src_ref=mean_send,
+                dst_ref=mean_recv.at[number],
+                send_sem=mean_send_sem,
+                recv_sem=mean_recv_sem.at[number],
+                device_id=(0, 0, 0),
+                device_id_type=MESH,
+            ).start()
+
+    @pl.when(first)
+    def _():
+        inter[...] = jnp.zeros(inter.shape, jnp.float32)
+        for gx_at in range(gx_count):
+            total = jnp.zeros((16, LANES), jnp.float32)
+            for gy_at in range(gy_count):
+                if gx_at or gy_at:
+                    mean_copy(gx_at, gy_at).wait_recv()
+                    total = total + mean_recv[gx_at * gy_count + gy_at]
+                else:
+                    total = total + mean_send[...]
+            for part in range(3):
+                inter[part, gx_at * piece_x : (gx_at + 1) * piece_x, :] = total[
+                    part * piece_x : (part + 1) * piece_x
+                ]
+        touched = cells_x + EDGE
+        for low in range(0, touched, EDGE):
+            film_start(low, EDGE, True)
+        for low in range(0, touched, EDGE):
+            film_end(low, EDGE, True)
+        for other in others:
+            cell_copy(*other).wait_send()
+
+    @pl.when((region == 0) & not_first)
+    def _():
+        mean_copy(0, 0).wait_send()
+
+    for turn in range(ROUNDS):
+        for way in range(6):
+
+            @pl.when(places[way][0])
+            def _(turn=turn, way=way):
+                halo_copy(turn, way, way ^ 1).wait_send()
+
+    for turn in range(2):
+        for way in range(4):
+
+            @pl.when(film_places[way][0])
+            def _(turn=turn, way=way):
+                film_copy(turn, way, way ^ 1).wait_send()
+
+
+def body(spins, uniforms, trials, exch_kernel, film_m, film_anis):
+    counts = tuple(lax.axis_size(axis) for axis in ("region", "gx", "gy"))
+    if not kernel_fits(spins, film_m, counts):
+        return body_general(spins, uniforms, trials, exch_kernel, film_m, film_anis)
+    regions, gx_count, gy_count = counts
+    _, layers, rows, _ = spins.shape
+    _, film_rows, film_cols = film_m.shape
+    cells_x = rows // K * gx_count
+    tiles = gx_count * gy_count
+    dma = pltpu.SemaphoreType.DMA
+
+    def vmem(*shape):
+        return pltpu.VMEM(shape, jnp.float32)
+
+    anywhere = pl.BlockSpec(memory_space=pl.ANY)
+    inside = pl.BlockSpec(memory_space=pltpu.VMEM)
+    return pl.pallas_call(
+        functools.partial(fused_kernel, counts),
+        out_shape=(
+            jax.ShapeDtypeStruct(spins.shape, jnp.float32),
+            jax.ShapeDtypeStruct(film_m.shape, jnp.float32),
+        ),
+        in_specs=[pl.BlockSpec(memory_space=pltpu.SMEM)] + [anywhere] * 5,
+        out_specs=(inside, inside),
+        scratch_shapes=[
+            vmem(ROUNDS, 3, layers, rows + 2 * EDGE, LANES),
+            vmem(*uniforms.shape),
+            vmem(*trials.shape),
+            vmem(3, rows, LANES),
+            vmem(3, film_rows + 2 * EDGE, film_cols),
+            vmem(3, film_rows + 2 * EDGE, film_cols),
+            vmem(3, film_rows, film_cols),
+            vmem(film_rows, film_cols),
+            vmem(ROUNDS, 2, EDGE, LANES),
+            vmem(ROUNDS, 2, EDGE, LANES),
+            vmem(ROUNDS, 2, rows, LANES),
+            vmem(ROUNDS, 2, rows, LANES),
+            vmem(ROUNDS, 2, 3, rows, LANES),
+            vmem(2, 2, EDGE, film_cols),
+            vmem(2, 2, EDGE, film_cols),
+            vmem(2, 2, film_rows, LANES),
+            vmem(2, 2, film_rows, LANES),
+            vmem(cells_x, LANES),
+            vmem(EDGE, LANES),
+            vmem(16, LANES),
+            vmem(tiles, 16, LANES),
+            vmem(3, cells_x + EDGE, LANES),
+            dma((5,)),
+            dma((ROUNDS, 6)),
+            dma((ROUNDS, 6)),
+            dma((2, 4)),
+            dma((2, 4)),
+            dma((regions * tiles,)),
+            dma,
+            dma,
+            dma((tiles,)),
+        ],
+        compiler_params=pltpu.CompilerParams(
+            collective_id=0, has_side_effects=True, vmem_limit_bytes=32 * 1024 * 1024
+        ),
+    )(exch_kernel.reshape(27), spins, uniforms, trials, film_m, film_anis)
+
+
 def solution(mesh):
     return jax.shard_map(
         body,

time: 296 us -> 35.9 us (0.12); the launches traced: 290 us -> 35.6 us
  other arithmetic: 137 us -> 0 us
  starting transfers between devices: 82.1 us -> 0 us
  blocking collectives: 52.3 us -> 0 us
  Pallas kernels: 0 us -> 28.2 us
  waiting for transfers between devices: 9.92 us -> 0 us
    add x49 -> x0, other arithmetic: 133 us -> none  [the longest x23 72.3 us: apply_transposed(): matrix[0, component] * vector[0] + matrix[1, component] * vector[1]]
    ppermute x32 -> x0, starting transfers between devices: 82.1 us -> none  [the longest x16 61.4 us: extended(): lax.ppermute(tail, axis, [(i, (i + 1) % count) for i in range(ends)])]
    psum x1 -> x0, blocking collectives: 41.8 us -> none  [spread(): return lax.psum(kept, axis)]
    pallas_call x0 -> x1, Pallas kernels: none -> 28.2 us  [body(): pl.pallas_call(functools.partial(fused_kernel, counts), out_shape=(jax.Sh...]
    all_gather x1 -> x0, blocking collectives: 10.6 us -> none  [body(): gathered = lax.all_gather(averages[None], ('gx', 'gy'), axis=0, tiled=True)]
    ppermute x32 -> x0, waiting for transfers between devices: 9.92 us -> none  [the longest x16 8.25 us: extended(): lax.ppermute(head, axis, [((i + 1) % count, i) for i in range(ends)])]
    slice x16 -> x0, local copies, waits for them, and re-layouts: 2.97 us -> none  [the longest x11 1.38 us: extended(): lax.slice_in_dim(cells, cells.shape[dim] - width, cells.shape[dim], axis=...]
    unnamed x15 -> x12, local copies, waits for them, and re-layouts: 3.39 us -> 5.95 us
  transfers between devices with their start and end apart: 32 -> 0, of which waited for: 5 -> 0; matrix products, arithmetic and copies ran while one was open for 43% -> 0% of each run, Pallas kernels for 0% -> 0%
where the time goes in v1:
time: 35.9 us; the launch traced here: 35.6 us
  Pallas kernels  28.2 us (79%)
  local copies, waits for them, and re-layouts  6.72 us (19%)
  between operations  0.64 us (2%)
    pallas_call x1, Pallas kernels, body(): pl.pallas_call(functools.partial(fused_kernel, counts), out_shape=(jax.Sh...  28.2 us
    unnamed x12, local copies, waits for them, and re-layouts  5.95 us
    reshape x1, local copies, waits for them, and re-layouts, body(): exch_kernel.reshape(27)  0.78 us

profile of v1, /device:TPU:0, one launch (start us, length us, event | category | flops | bytes accessed | tf_op | source)
XLA Modules:
  0.0 35.6 jit_solution(14117078112029904819)
XLA Ops:
  0.6 0.8 %reshape.7.exch = f32[27]{0:T(128)S(1)} reshape(f32[3,3,3]{2,1,0:T(4,128)} %param.9) | data formatting | bytes 216 | tf_op jit(solution)/shard_map/reshape | solution.py:744
  1.4 0.0 copy-start
  1.4 1.0 %copy-done = f32[3,128,256]{2,1,0:T(8,128)S(1)} copy-done((f32[3,128,256]{2,1,0:T(8,128)S(1)}, f32[3,128,256]{2,1,0:T(8,128)}, u32[]{:S(2)}) %copy-start) | copy-done | bytes 393240
  2.4 0.0 copy-start.1
  2.4 0.9 %copy-done.1 = f32[2,3,2,32,128]{4,3,2,1,0:T(8,128)S(1)} copy-done((f32[2,3,2,32,128]{4,3,2,1,0:T(8,128)S(1)}, f32[2,3,2,32,128]{4,3,2,1,0:T(8,128)}, u32[]{:S(2)}) %copy-start.1) | copy-done | bytes 196632
  3.3 0.0 copy-start.2
  3.3 0.9 %copy-done.2 = f32[128,256]{1,0:T(8,128)S(1)} copy-done((f32[128,256]{1,0:T(8,128)S(1)}, f32[128,256]{1,0:T(8,128)}, u32[]{:S(2)}) %copy-start.2) | copy-done | bytes 131096
  4.2 0.0 copy-start.3
  4.2 0.9 %copy-done.3 = f32[3,2,32,128]{3,2,1,0:T(8,128)S(1)} copy-done((f32[3,2,32,128]{3,2,1,0:T(8,128)S(1)}, f32[3,2,32,128]{3,2,1,0:T(8,128)}, u32[]{:S(2)}) %copy-start.3) | copy-done | bytes 98328
  5.1 0.0 copy-start.4
  5.1 0.8 %copy-done.4 = f32[2,2,32,128]{3,2,1,0:T(8,128)S(1)} copy-done((f32[2,2,32,128]{3,2,1,0:T(8,128)S(1)}, f32[2,2,32,128]{3,2,1,0:T(8,128)}, u32[]{:S(2)}) %copy-start.4) | copy-done | bytes 65560
  6.0 28.2 %shard_map.77 = (f32[3,2,32,128]{3,2,1,0:T(8,128)S(1)}, f32[3,128,256]{2,1,0:T(8,128)S(1)}) custom-call(f32[27]{0:T(128)S(1)} %reshape.7.exch, f32[3,2,32,128]{3,2,1,0:T(8,128)S(1)} %copy-done.3, f32[2,2,32,128]{3,2,1,0:T(8,128)S(1)} %copy-done.4, f32[2,3,2,32,128]{4,3,2,1,0:T(8,128)S(1)} %copy-done.1, f32[3,128,256]{2,1,0:T(8,128)S(1)} %copy-done, ...), custom_call_target="tpu_custom_call" | custom-call | tf_op jit(solution)/shard_map/pallas_call | solution.py:700
  34.2 0.6 %copy.10 = f32[3,2,32,128]{3,2,1,0:T(8,128)} copy(f32[3,2,32,128]{3,2,1,0:T(8,128)S(1)} %get-tuple-element.4) | data formatting | bytes 196608
  34.8 0.7 %copy.11 = f32[3,128,256]{2,1,0:T(8,128)} copy(f32[3,128,256]{2,1,0:T(8,128)S(1)} %get-tuple-element.5) | data formatting | bytes 786432
Async XLA Ops:
  1.4 1.0 %copy-start = (f32[3,128,256]{2,1,0:T(8,128)S(1)}, f32[3,128,256]{2,1,0:T(8,128)}, u32[]{:S(2)}) copy-start(f32[3,128,256]{2,1,0:T(8,128)} %film_hbm.1) | copy-start | bytes 1179652
  2.4 0.9 %copy-start.1 = (f32[2,3,2,32,128]{4,3,2,1,0:T(8,128)S(1)}, f32[2,3,2,32,128]{4,3,2,1,0:T(8,128)}, u32[]{:S(2)}) copy-start(f32[2,3,2,32,128]{4,3,2,1,0:T(8,128)} %trial_hbm.1) | copy-start | bytes 589828
  3.3 0.9 %copy-start.2 = (f32[128,256]{1,0:T(8,128)S(1)}, f32[128,256]{1,0:T(8,128)}, u32[]{:S(2)}) copy-start(f32[128,256]{1,0:T(8,128)} %anis_hbm.1) | copy-start | bytes 393220
  4.2 0.9 %copy-start.3 = (f32[3,2,32,128]{3,2,1,0:T(8,128)S(1)}, f32[3,2,32,128]{3,2,1,0:T(8,128)}, u32[]{:S(2)}) copy-start(f32[3,2,32,128]{3,2,1,0:T(8,128)} %spins_hbm.1) | copy-start | bytes 294916
  5.1 0.8 %copy-start.4 = (f32[2,2,32,128]{3,2,1,0:T(8,128)S(1)}, f32[2,2,32,128]{3,2,1,0:T(8,128)}, u32[]{:S(2)}) copy-start(f32[2,2,32,128]{3,2,1,0:T(8,128)} %unif_hbm.1) | copy-start | bytes 196612

commit v2 on v1

--- a/solution.py
+++ b/solution.py
@@ -248,6 +248,7 @@
     fy_recv,
     cell_all,
     cell_own,
+    cell_wide,
     mean_send,
     mean_recv,
     inter,
@@ -256,6 +257,8 @@
     recv_sem,
     film_send_sem,
     film_recv_sem,
+    block_send_sem,
+    block_recv_sem,
     cell_send_sem,
     cell_recv_sem,
     mean_send_sem,
@@ -274,6 +277,7 @@
     gy = lax.axis_index("gy")
     first = (region == 0) & (gx == 0) & (gy == 0)
     not_first = jnp.logical_not(first)
+    leader = (gx == 0) & (gy == 0)
 
     places = [
         (region > 0, (region - 1, gx, gy)),
@@ -313,7 +317,11 @@
         def _(place=place):
             pl.semaphore_signal(barrier, inc=1, device_id=place, device_id_type=MESH)
 
-    @pl.when(not_first)
+    @pl.when(jnp.logical_not(leader))
+    def _():
+        pl.semaphore_signal(barrier, inc=1, device_id=(region, 0, 0), device_id_type=MESH)
+
+    @pl.when(leader & not_first)
     def _():
         pl.semaphore_signal(barrier, inc=1, device_id=(0, 0, 0), device_id_type=MESH)
 
@@ -463,7 +471,7 @@
 
     x_iota = lax.broadcasted_iota(jnp.int32, (rows, LANES), 0)
 
-    def half_sweep(turn):
+    def half_sweep(turn, send_mean):
         sweep, colour = turn // 2, turn % 2
         for layer in range(layers):
             own = [stack[turn, part, layer, inner, :] for part in range(3)]
@@ -485,8 +493,8 @@
                 field = coupling_down * film_near[part]
                 for way in range(3):
                     for other in range(3):
-                        field = field + exch[9 * way + 3 * part + other] * around[2 * way + 1][other]
-                        field = field + exch[9 * way + 3 * other + part] * around[2 * way][other]
+                        field = field + exch[way, part, other] * around[2 * way + 1][other]
+                        field = field + exch[way, other, part] * around[2 * way][other]
                 gain = gain + shift[part] * field
             change = -gain - anisotropy * (proposal[2] * proposal[2] - own[2] * own[2])
             accept = jnp.exp(jnp.minimum(-inverse_temp * change, 0.0))
@@ -499,24 +507,40 @@
                     spins_out[part, layer] = fresh
                 else:
                     stack[turn + 1, part, layer, inner, :] = fresh
-
-    def cell_copy(region_at, gx_at, gy_at):
-        number = (region_at * gx_count + gx_at) * gy_count + gy_at
+            if turn == ROUNDS - 1:
+                if layer == 0:
+                    send_mean()
+            else:
+                if layer == 0:
+                    send_halo(turn + 1, [0])
+                if layer == layers - 1:
+                    send_halo(turn + 1, [1])
+
+    def block_copy(region_at):
+        return pltpu.make_async_remote_copy(
+            src_ref=cell_all,
+            dst_ref=cell_all,
+            send_sem=block_send_sem.at[region_at],
+            recv_sem=block_recv_sem,
+            device_id=(region_at, 0, 0),
+            device_id_type=MESH,
+        )
+
+    def cell_copy(gx_at, gy_at):
         return pltpu.make_async_remote_copy(
             src_ref=cell_all.at[pl.ds(gx_at // per_tile * EDGE, EDGE), :],
             dst_ref=cell_own,
-            send_sem=cell_send_sem.at[number],
+            send_sem=cell_send_sem.at[gx_at * gy_count + gy_at],
             recv_sem=cell_recv_sem,
-            device_id=(region_at, gx_at, gy_at),
+            device_id=(region, gx_at, gy_at),
             device_id_type=MESH,
         )
 
-    others = [
-        (region_at, gx_at, gy_at)
-        for region_at in reversed(range(regions))
+    members = [
+        (gx_at, gy_at)
         for gx_at in reversed(range(gx_count))
         for gy_at in reversed(range(gy_count))
-        if region_at or gx_at or gy_at
+        if gx_at or gy_at
     ]
 
     def mean_copy(gx_at, gy_at):
@@ -558,86 +582,98 @@
             moved = pltpu.roll(film[part, EDGE : EDGE + cells_x, :LANES], part * cells_y, 1)
             packed = jnp.where(cell_lane >= part * cells_y, moved, packed)
         cell_all[...] = packed
-        cell_own[...] = packed[:EDGE]
 
     pack_film(0, film)
 
     expected = sum(there.astype(jnp.int32) for there, _ in places + film_places[:2])
-    expected = expected + jnp.where(
-        first, regions * gx_count * gy_count - 1, jnp.where(region == 0, 1, 0)
-    )
+    expected = expected + jnp.where(leader, gx_count * gy_count - 1, jnp.where(region == 0, 1, 0))
+    expected = expected + jnp.where(first, regions - 1, 0)
     pl.semaphore_wait(barrier, expected)
 
     @pl.when(first)
     def _():
-        for other in others:
-            cell_copy(*other).start()
+        for region_at in reversed(range(1, regions)):
+            block_copy(region_at).start()
+        for member in members:
+            cell_copy(*member).start()
 
     send_halo(0, range(6))
     send_film(0)
+
+    @pl.when(leader & not_first)
+    def _():
+        block_copy(0).wait_recv()
+        for member in members:
+            cell_copy(*member).start()
+
+    row_at = lax.broadcasted_iota(jnp.int32, (LANES, LANES), 0)
+    col_at = lax.broadcasted_iota(jnp.int32, (LANES, LANES), 1)
+    dot = functools.partial(jnp.dot, precision=lax.Precision.HIGHEST, preferred_element_type=jnp.float32)
+    film_steps = list(range(0, film_rows, 16))
     for load in loads[2:]:
         load.wait()
-
-    @pl.when(not_first)
-    def _():
-        cell_copy(0, 0, 0).wait_recv()
-
-    row_at = lax.broadcasted_iota(jnp.int32, (LANES, LANES), 0)
-    col_at = lax.broadcasted_iota(jnp.int32, (LANES, LANES), 1)
-    pick_row = lax.broadcasted_iota(jnp.int32, (rows, EDGE), 0) // K + gx % per_tile * piece_x
-    pick = (lax.broadcasted_iota(jnp.int32, (rows, EDGE), 1) == pick_row).astype(jnp.float32)
-    dot = functools.partial(jnp.dot, precision=lax.Precision.HIGHEST, preferred_element_type=jnp.float32)
-    cells = jnp.where(
-        lax.broadcasted_iota(jnp.int32, (EDGE, LANES), 1) < 3 * cells_y, cell_own[...], 0.0
-    )
-    tall = dot(pick, cells)
+    take_film(0, film)
+    for low in film_steps:
+        film_start(low, 16)
+    pack_film(1, trial_film)
+    send_film(1)
+
+    @pl.when(leader)
+    def _():
+        cell_own[...] = cell_all[:EDGE, :]
+
+    @pl.when(jnp.logical_not(leader))
+    def _():
+        cell_copy(0, 0).wait_recv()
+
+    cells = cell_own[...]
     for part in range(3):
         spread_cols = (row_at == part * cells_y + gy * piece_y + col_at // K).astype(jnp.float32)
-        film_near[part] = dot(tall, spread_cols)
-
-    film_steps = list(range(0, film_rows, 16))
+        cell_wide[part] = dot(cells, spread_cols)
+    for part in range(3):
+        for at in range(piece_x):
+            line_at = cell_wide[part, pl.ds(gx % per_tile * piece_x + at, 1), :]
+            film_near[part, at * K : (at + 1) * K, :] = jnp.broadcast_to(line_at, (K, LANES))
+
+    def send_mean():
+        @pl.when(region == 0)
+        def _():
+            for part in range(3):
+                for at in range(piece_x):
+                    block = spins_out[part, 0, at * K : (at + 1) * K, :]
+                    place = part * piece_x + at
+                    mean_send[place : place + 1, :] = jnp.sum(block, axis=0, keepdims=True)
+            for at in range(3 * piece_x, 16):
+                mean_send[at : at + 1, :] = jnp.zeros((1, LANES), jnp.float32)
+            gather_cols = jnp.where(col_at == row_at // K + gy * piece_y, 1.0 / (K * K), 0.0)
+            mean_send[...] = dot(mean_send[...], gather_cols)
+
+            @pl.when(not_first)
+            def _():
+                number = gx * gy_count + gy
+                pltpu.make_async_remote_copy(
+                    src_ref=mean_send,
+                    dst_ref=mean_recv.at[number],
+                    send_sem=mean_send_sem,
+                    recv_sem=mean_recv_sem.at[number],
+                    device_id=(0, 0, 0),
+                    device_id_type=MESH,
+                ).start()
+
+    half = len(film_steps) // 2
     for turn in range(ROUNDS):
         take_halo(turn)
-        half_sweep(turn)
+        half_sweep(turn, send_mean)
         if turn + 1 < ROUNDS:
             pack_halo(turn + 1)
-            send_halo(turn + 1, range(6))
+            send_halo(turn + 1, range(2, 6))
         if turn == 0:
-            take_film(0, film)
-            for low in film_steps:
-                film_start(low, 16)
-            pack_film(1, trial_film)
-            send_film(1)
+            take_film(1, trial_film)
+            for low in film_steps[:half]:
+                film_end(low, 16)
         if turn == 1:
-            take_film(1, trial_film)
-            for low in film_steps[: len(film_steps) // 2]:
+            for low in film_steps[half:]:
                 film_end(low, 16)
-        if turn == 2:
-            for low in film_steps[len(film_steps) // 2 :]:
-                film_end(low, 16)
-
-    @pl.when(region == 0)
-    def _():
-        for part in range(3):
-            for at in range(piece_x):
-                block = spins_out[part, 0, at * K : (at + 1) * K, :]
-                mean_send[part * piece_x + at : part * piece_x + at + 1, :] = jnp.sum(block, axis=0, keepdims=True)
-        for at in range(3 * piece_x, 16):
-            mean_send[at : at + 1, :] = jnp.zeros((1, LANES), jnp.float32)
-        gather_cols = jnp.where(col_at == row_at // K + gy * piece_y, 1.0 / (K * K), 0.0)
-        mean_send[...] = dot(mean_send[...], gather_cols)
-
-        @pl.when(not_first)
-        def _():
-            number = gx * gy_count + gy
-            pltpu.make_async_remote_copy(
-                src_ref=mean_send,
-                dst_ref=mean_recv.at[number],
-                send_sem=mean_send_sem,
-                recv_sem=mean_recv_sem.at[number],
-                device_id=(0, 0, 0),
-                device_id_type=MESH,
-            ).start()
 
     @pl.when(first)
     def _():
@@ -654,13 +690,15 @@
                 inter[part, gx_at * piece_x : (gx_at + 1) * piece_x, :] = total[
                     part * piece_x : (part + 1) * piece_x
                 ]
-        touched = cells_x + EDGE
-        for low in range(0, touched, EDGE):
-            film_start(low, EDGE, True)
-        for low in range(0, touched, EDGE):
-            film_end(low, EDGE, True)
-        for other in others:
-            cell_copy(*other).wait_send()
+        film_start(0, cells_x, True)
+        film_end(0, cells_x + EDGE, True)
+        for region_at in range(1, regions):
+            block_copy(region_at).wait_send()
+
+    @pl.when(leader)
+    def _():
+        for member in members:
+            cell_copy(*member).wait_send()
 
     @pl.when((region == 0) & not_first)
     def _():
@@ -695,7 +733,7 @@
     def vmem(*shape):
         return pltpu.VMEM(shape, jnp.float32)
 
-    anywhere = pl.BlockSpec(memory_space=pl.ANY)
+    anywhere = pl.BlockSpec(memory_space=pltpu.HBM)
     inside = pl.BlockSpec(memory_space=pltpu.VMEM)
     return pl.pallas_call(
         functools.partial(fused_kernel, counts),
@@ -725,6 +763,7 @@
             vmem(2, 2, film_rows, LANES),
             vmem(cells_x, LANES),
             vmem(EDGE, LANES),
+            vmem(3, EDGE, LANES),
             vmem(16, LANES),
             vmem(tiles, 16, LANES),
             vmem(3, cells_x + EDGE, LANES),
@@ -733,15 +772,17 @@
             dma((ROUNDS, 6)),
             dma((2, 4)),
             dma((2, 4)),
-            dma((regions * tiles,)),
+            dma((regions,)),
+            dma,
+            dma((tiles,)),
             dma,
             dma,
             dma((tiles,)),
         ],
         compiler_params=pltpu.CompilerParams(
-            collective_id=0, has_side_effects=True, vmem_limit_bytes=32 * 1024 * 1024
+            collective_id=0, has_side_effects=True, vmem_limit_bytes=60 * 1024 * 1024
         ),
-    )(exch_kernel.reshape(27), spins, uniforms, trials, film_m, film_anis)
+    )(exch_kernel, spins, uniforms, trials, film_m, film_anis)
 
 
 def solution(mesh):

time: 35.9 us -> 32.1 us (0.89)
  local copies, waits for them, and re-layouts: 6.72 us -> 3.31 us
    unnamed x12 -> x2, local copies, waits for them, and re-layouts: 5.95 us -> 3.31 us
    reshape x1 -> x0, local copies, waits for them, and re-layouts: 0.78 us -> none  [body(): exch_kernel.reshape(27)]
where the time goes in v2:
time: 32.1 us; the launch traced here: 31.9 us
  Pallas kernels  27.9 us (87%)
  local copies, waits for them, and re-layouts  3.31 us (10%)
  between operations  0.64 us (2%)
    pallas_call x1, Pallas kernels, body(): pl.pallas_call(functools.partial(fused_kernel, counts), out_shape=(jax.Sh...  27.9 us
    unnamed x2, local copies, waits for them, and re-layouts  3.31 us

profile of v2, /device:TPU:0, one launch (start us, length us, event | category | flops | bytes accessed | tf_op | source)
XLA Modules:
  0.0 31.9 jit_solution(2428943037239114839)
XLA Ops:
  0.6 27.9 %shard_map.77 = (f32[3,2,32,128]{3,2,1,0:T(8,128)}, f32[3,128,256]{2,1,0:T(8,128)}) custom-call(f32[3,3,3]{2,1,0:T(4,128)} %exch.1, f32[3,2,32,128]{3,2,1,0:T(8,128)} %spins_hbm.1, f32[2,2,32,128]{3,2,1,0:T(8,128)} %unif_hbm.1, f32[2,3,2,32,128]{4,3,2,1,0:T(8,128)} %trial_hbm.1, f32[3,128,256]{2,1,0:T(8,128)} %film_hbm.1, f32[128,256]{1,0:T(8,128)} %anis_hbm.1), custom_call_target="tpu_custom_call" | custom-call | tf_op jit(solution)/shard_map/pallas_call | solution.py:738
  28.6 1.5 %copy.10 = f32[3,2,32,128]{3,2,1,0:T(8,128)} copy(f32[3,2,32,128]{3,2,1,0:T(8,128)} %get-tuple-element.4) | data formatting | bytes 196608
  30.1 1.8 %copy.11 = f32[3,128,256]{2,1,0:T(8,128)} copy(f32[3,128,256]{2,1,0:T(8,128)} %get-tuple-element.5) | data formatting | bytes 786432

commit v3 on v2

--- a/solution.py
+++ b/solution.py
@@ -435,23 +435,25 @@
         repeat = film_cols // LANES
         magnet, field = [], []
         for part in range(3):
-            at = EDGE + low
-            block = source[part, at : at + count, :]
-            before = pltpu.roll(fy_recv[turn, 0, low : low + count, :], (LANES - part) % LANES, 1) if part else fy_recv[turn, 0, low : low + count, :]
-            after = pltpu.roll(fy_recv[turn, 1, low : low + count, :], LANES - 1 - part, 1)
-            total = source[part, at - 1 : at - 1 + count, :] + source[part, at + 1 : at + 1 + count, :]
+            tall = source[part, pl.ds(low, count + 2 * EDGE), :]
+            span = count + 2 * EDGE
+            block = tall[EDGE : EDGE + count]
+            before = fy_recv[turn, 0, pl.ds(low, count), :]
+            before = pltpu.roll(before, LANES - part, 1) if part else before
+            after = pltpu.roll(fy_recv[turn, 1, pl.ds(low, count), :], LANES - 1 - part, 1)
+            total = (pltpu.roll(tall, 1, 0) + pltpu.roll(tall, span - 1, 0))[EDGE : EDGE + count]
             total = total + jnp.where(wide == 0, jnp.concatenate([before] * repeat, 1), pltpu.roll(block, 1, 1))
             total = total + jnp.where(
                 wide == film_cols - 1, jnp.concatenate([after] * repeat, 1), pltpu.roll(block, film_cols - 1, 1)
             )
             total = total - 4.0 * block
             if with_inter:
-                extra = coupling_up * inter[part, low : low + count, :]
+                extra = coupling_up * inter[part, pl.ds(low, count), :]
                 rest = [jnp.zeros((count, LANES), jnp.float32)] * (repeat - 1)
                 total = total + jnp.concatenate([extra] + rest, 1)
             magnet.append(block)
             field.append(total)
-        field[2] = field[2] + anis[low : low + count, :] * magnet[2]
+        field[2] = field[2] + anis[pl.ds(low, count), :] * magnet[2]
         precession = cross(magnet, field)
         relaxation = cross(magnet, precession)
         factor = -1.0 / (1.0 + damping * damping)
@@ -460,18 +462,18 @@
     def film_start(low, count, with_inter=False):
         magnet, speed = rate(0, film, low, count, with_inter)
         for part in range(3):
-            trial_film[part, EDGE + low : EDGE + low + count, :] = magnet[part] + time_step * speed[part]
-            half_film[part, low : low + count, :] = magnet[part] + (0.5 * time_step) * speed[part]
+            trial_film[part, pl.ds(low + EDGE, count), :] = magnet[part] + time_step * speed[part]
+            half_film[part, pl.ds(low, count), :] = magnet[part] + (0.5 * time_step) * speed[part]
 
     def film_end(low, count, with_inter=False):
         _, speed = rate(1, trial_film, low, count, with_inter)
-        result = unit([half_film[part, low : low + count, :] + (0.5 * time_step) * speed[part] for part in range(3)])
+        result = unit([half_film[part, pl.ds(low, count), :] + (0.5 * time_step) * speed[part] for part in range(3)])
         for part in range(3):
-            film_out[part, low : low + count, :] = result[part]
+            film_out[part, pl.ds(low, count), :] = result[part]
 
     x_iota = lax.broadcasted_iota(jnp.int32, (rows, LANES), 0)
 
-    def half_sweep(turn, send_mean):
+    def half_sweep(turn, send_mean, last):
         sweep, colour = turn // 2, turn % 2
         for layer in range(layers):
             own = [stack[turn, part, layer, inner, :] for part in range(3)]
@@ -503,11 +505,11 @@
             parity = (region * layers + layer + gx * rows + gy * LANES + x_iota + lane) % 2
             for part in range(3):
                 fresh = jnp.where(parity == colour, blended[part], own[part])
-                if turn == ROUNDS - 1:
+                if last:
                     spins_out[part, layer] = fresh
                 else:
                     stack[turn + 1, part, layer, inner, :] = fresh
-            if turn == ROUNDS - 1:
+            if last:
                 if layer == 0:
                     send_mean()
             else:
@@ -609,12 +611,19 @@
     row_at = lax.broadcasted_iota(jnp.int32, (LANES, LANES), 0)
     col_at = lax.broadcasted_iota(jnp.int32, (LANES, LANES), 1)
     dot = functools.partial(jnp.dot, precision=lax.Precision.HIGHEST, preferred_element_type=jnp.float32)
-    film_steps = list(range(0, film_rows, 16))
+    film_steps = film_rows // 16
+
+    def film_run(step, start, stop):
+        def one(at, carry):
+            step(pl.multiple_of(at * 16, 16), 16)
+            return carry
+
+        lax.fori_loop(start, stop, one, 0)
+
     for load in loads[2:]:
         load.wait()
     take_film(0, film)
-    for low in film_steps:
-        film_start(low, 16)
+    film_run(film_start, 0, film_steps)
     pack_film(1, trial_film)
     send_film(1)
 
@@ -660,20 +669,27 @@
                     device_id_type=MESH,
                 ).start()
 
-    half = len(film_steps) // 2
-    for turn in range(ROUNDS):
+    half = film_steps // 2
+
+    def round_of(turn, carry):
         take_halo(turn)
-        half_sweep(turn, send_mean)
-        if turn + 1 < ROUNDS:
-            pack_halo(turn + 1)
-            send_halo(turn + 1, range(2, 6))
-        if turn == 0:
+        half_sweep(turn, send_mean, False)
+        pack_halo(turn + 1)
+        send_halo(turn + 1, range(2, 6))
+
+        @pl.when(turn == 0)
+        def _():
             take_film(1, trial_film)
-            for low in film_steps[:half]:
-                film_end(low, 16)
-        if turn == 1:
-            for low in film_steps[half:]:
-                film_end(low, 16)
+
+        @pl.when(turn < 2)
+        def _():
+            film_run(film_end, turn * half, half + turn * (film_steps - half))
+
+        return carry
+
+    lax.fori_loop(0, ROUNDS - 1, round_of, 0)
+    take_halo(ROUNDS - 1)
+    half_sweep(ROUNDS - 1, send_mean, True)
 
     @pl.when(first)
     def _():
@@ -704,12 +720,16 @@
     def _():
         mean_copy(0, 0).wait_send()
 
-    for turn in range(ROUNDS):
+    def settle(turn, carry):
         for way in range(6):
 
             @pl.when(places[way][0])
-            def _(turn=turn, way=way):
+            def _(way=way):
                 halo_copy(turn, way, way ^ 1).wait_send()
+
+        return carry
+
+    lax.fori_loop(0, ROUNDS, settle, 0)
 
     for turn in range(2):
         for way in range(4):

time: 32.1 us -> 32.1 us (level)
  no operation moved by 1% of the time
where the time goes in v3:
time: 32.1 us; the launch traced here: 31.8 us
  Pallas kernels  27.9 us (87%)
  local copies, waits for them, and re-layouts  3.31 us (10%)
  between operations  0.64 us (2%)
    pallas_call x1, Pallas kernels, body(): pl.pallas_call(functools.partial(fused_kernel, counts), out_shape=(jax.Sh...  27.9 us
    unnamed x2, local copies, waits for them, and re-layouts  3.31 us

profile of v3, /device:TPU:0, one launch (start us, length us, event | category | flops | bytes accessed | tf_op | source)
XLA Modules:
  0.0 31.8 jit_solution(2815063417178544261)
XLA Ops:
  0.6 27.9 %shard_map.77 = (f32[3,2,32,128]{3,2,1,0:T(8,128)}, f32[3,128,256]{2,1,0:T(8,128)}) custom-call(f32[3,3,3]{2,1,0:T(4,128)} %exch.1, f32[3,2,32,128]{3,2,1,0:T(8,128)} %spins_hbm.1, f32[2,2,32,128]{3,2,1,0:T(8,128)} %unif_hbm.1, f32[2,3,2,32,128]{4,3,2,1,0:T(8,128)} %trial_hbm.1, f32[3,128,256]{2,1,0:T(8,128)} %film_hbm.1, f32[128,256]{1,0:T(8,128)} %anis_hbm.1), custom_call_target="tpu_custom_call" | custom-call | tf_op jit(solution)/shard_map/pallas_call | solution.py:758
  28.5 1.5 %copy.10 = f32[3,2,32,128]{3,2,1,0:T(8,128)} copy(f32[3,2,32,128]{3,2,1,0:T(8,128)} %get-tuple-element.4) | data formatting | bytes 196608
  30.1 1.8 %copy.11 = f32[3,128,256]{2,1,0:T(8,128)} copy(f32[3,128,256]{2,1,0:T(8,128)} %get-tuple-element.5) | data formatting | bytes 786432

commit v4 on v3

--- a/solution.py
+++ b/solution.py
@@ -241,6 +241,7 @@
     x_recv,
     y_send,
     y_recv,
+    z_send,
     z_recv,
     fx_send,
     fx_recv,
@@ -337,8 +338,7 @@
 
     def halo(turn, way):
         if way < 2:
-            source = stack.at[turn, :, 0 if way == 0 else layers - 1, inner, :]
-            return source, z_recv
+            return z_send.at[turn, way], z_recv
         if way < 4:
             return x_send.at[turn, way - 2], x_recv
         return y_send.at[turn, way - 4], y_recv
@@ -364,6 +364,21 @@
             device_id=film_places[way][1],
             device_id_type=MESH,
         )
+
+    half_rows = rows // 2
+    x_iota = lax.broadcasted_iota(jnp.int32, (rows, LANES), 0)
+
+    def parity_of(layer):
+        return (region * layers + layer + gx * rows + gy * LANES + x_iota + lane) % 2
+
+    def pack_face(turn, way, blocks, needed):
+        for part in range(3):
+            shifted = pltpu.roll(blocks[part][half_rows:], 1, 1)
+            z_send[turn, way, part] = jnp.where(needed[:half_rows], blocks[part][:half_rows], shifted)
+
+    def face(turn, way, part):
+        packed = z_recv[turn, way, part]
+        return jnp.concatenate([packed, pltpu.roll(packed, LANES - 1, 1)], 0)
 
     def pack_halo(turn):
         right = jnp.zeros((rows, LANES), jnp.float32)
@@ -471,8 +486,6 @@
         for part in range(3):
             film_out[part, pl.ds(low, count), :] = result[part]
 
-    x_iota = lax.broadcasted_iota(jnp.int32, (rows, LANES), 0)
-
     def half_sweep(turn, send_mean, last):
         sweep, colour = turn // 2, turn % 2
         for layer in range(layers):
@@ -481,8 +494,8 @@
             around = [[] for _ in range(6)]
             for part in range(3):
                 at = part * layers + layer
-                around[0].append(z_recv[turn, 0, part] if layer == 0 else stack[turn, part, layer - 1, inner, :])
-                around[1].append(z_recv[turn, 1, part] if layer == layers - 1 else stack[turn, part, layer + 1, inner, :])
+                around[0].append(face(turn, 0, part) if layer == 0 else stack[turn, part, layer - 1, inner, :])
+                around[1].append(face(turn, 1, part) if layer == layers - 1 else stack[turn, part, layer + 1, inner, :])
                 around[2].append(stack[turn, part, layer, EDGE - 1 : EDGE - 1 + rows, :])
                 around[3].append(stack[turn, part, layer, EDGE + 1 : EDGE + 1 + rows, :])
                 before = pltpu.roll(y_recv[turn, 0], LANES - at, 1) if at else y_recv[turn, 0]
@@ -502,9 +515,11 @@
             accept = jnp.exp(jnp.minimum(-inverse_temp * change, 0.0))
             weight = 1.0 / (1.0 + jnp.exp((unif[sweep, layer] - accept) * (1.0 / softness)))
             blended = unit([own[part] + weight * shift[part] for part in range(3)])
-            parity = (region * layers + layer + gx * rows + gy * LANES + x_iota + lane) % 2
+            chosen = parity_of(layer) == colour
+            faces = []
             for part in range(3):
-                fresh = jnp.where(parity == colour, blended[part], own[part])
+                fresh = jnp.where(chosen, blended[part], own[part])
+                faces.append(fresh)
                 if last:
                     spins_out[part, layer] = fresh
                 else:
@@ -514,8 +529,10 @@
                     send_mean()
             else:
                 if layer == 0:
+                    pack_face(turn + 1, 0, faces, chosen)
                     send_halo(turn + 1, [0])
                 if layer == layers - 1:
+                    pack_face(turn + 1, 1, faces, chosen)
                     send_halo(turn + 1, [1])
 
     def block_copy(region_at):
@@ -573,6 +590,9 @@
                 target[turn, way % 2] = jnp.zeros(target.shape[2:], jnp.float32)
 
     loads[0].wait()
+    for way, layer in enumerate((0, layers - 1)):
+        blocks = [stack[0, part, layer, inner, :] for part in range(3)]
+        pack_face(0, way, blocks, parity_of(layer) == 1)
     pack_halo(0)
     loads[1].wait()
 
@@ -776,7 +796,8 @@
             vmem(ROUNDS, 2, EDGE, LANES),
             vmem(ROUNDS, 2, rows, LANES),
             vmem(ROUNDS, 2, rows, LANES),
-            vmem(ROUNDS, 2, 3, rows, LANES),
+            vmem(ROUNDS, 2, 3, rows // 2, LANES),
+            vmem(ROUNDS, 2, 3, rows // 2, LANES),
             vmem(2, 2, EDGE, film_cols),
             vmem(2, 2, EDGE, film_cols),
             vmem(2, 2, film_rows, LANES),

time: 32.1 us -> 31.5 us (0.981)
  Pallas kernels: 27.9 us -> 27.3 us
    pallas_call x1, Pallas kernels: 27.9 us -> 27.3 us  [body(): pl.pallas_call(functools.partial(fused_kernel, counts), out_shape=(jax.Sh...]
where the time goes in v4:
time: 31.5 us; the launch traced here: 31.2 us
  Pallas kernels  27.3 us (87%)
  local copies, waits for them, and re-layouts  3.31 us (11%)
  between operations  0.64 us (2%)
    pallas_call x1, Pallas kernels, body(): pl.pallas_call(functools.partial(fused_kernel, counts), out_shape=(jax.Sh...  27.3 us
    unnamed x2, local copies, waits for them, and re-layouts  3.31 us

profile of v4, /device:TPU:0, one launch (start us, length us, event | category | flops | bytes accessed | tf_op | source)
XLA Modules:
  0.0 31.2 jit_solution(5561154584042376249)
XLA Ops:
  0.6 27.3 %shard_map.77 = (f32[3,2,32,128]{3,2,1,0:T(8,128)}, f32[3,128,256]{2,1,0:T(8,128)}) custom-call(f32[3,3,3]{2,1,0:T(4,128)} %exch.1, f32[3,2,32,128]{3,2,1,0:T(8,128)} %spins_hbm.1, f32[2,2,32,128]{3,2,1,0:T(8,128)} %unif_hbm.1, f32[2,3,2,32,128]{4,3,2,1,0:T(8,128)} %trial_hbm.1, f32[3,128,256]{2,1,0:T(8,128)} %film_hbm.1, f32[128,256]{1,0:T(8,128)} %anis_hbm.1), custom_call_target="tpu_custom_call" | custom-call | tf_op jit(solution)/shard_map/pallas_call | solution.py:778
  27.9 1.5 %copy.10 = f32[3,2,32,128]{3,2,1,0:T(8,128)} copy(f32[3,2,32,128]{3,2,1,0:T(8,128)} %get-tuple-element.4) | data formatting | bytes 196608
  29.5 1.8 %copy.11 = f32[3,128,256]{2,1,0:T(8,128)} copy(f32[3,128,256]{2,1,0:T(8,128)} %get-tuple-element.5) | data formatting | bytes 786432

commit v5 on v4

--- a/solution.py
+++ b/solution.py
@@ -605,8 +605,6 @@
             packed = jnp.where(cell_lane >= part * cells_y, moved, packed)
         cell_all[...] = packed
 
-    pack_film(0, film)
-
     expected = sum(there.astype(jnp.int32) for there, _ in places + film_places[:2])
     expected = expected + jnp.where(leader, gx_count * gy_count - 1, jnp.where(region == 0, 1, 0))
     expected = expected + jnp.where(first, regions - 1, 0)
@@ -620,6 +618,7 @@
             cell_copy(*member).start()
 
     send_halo(0, range(6))
+    pack_film(0, film)
     send_film(0)
 
     @pl.when(leader & not_first)
@@ -642,10 +641,6 @@
 
     for load in loads[2:]:
         load.wait()
-    take_film(0, film)
-    film_run(film_start, 0, film_steps)
-    pack_film(1, trial_film)
-    send_film(1)
 
     @pl.when(leader)
     def _():
@@ -699,11 +694,18 @@
 
         @pl.when(turn == 0)
         def _():
+            take_film(0, film)
+            film_run(film_start, 0, film_steps)
+            pack_film(1, trial_film)
+            send_film(1)
+
+        @pl.when(turn == 1)
+        def _():
             take_film(1, trial_film)
 
-        @pl.when(turn < 2)
+        @pl.when(turn > 0)
         def _():
-            film_run(film_end, turn * half, half + turn * (film_steps - half))
+            film_run(film_end, (turn - 1) * half, half + (turn - 1) * (film_steps - half))
 
         return carry
 

time: 31.5 us -> 31.5 us (level)
  no operation moved by 1% of the time
where the time goes in v5:
time: 31.5 us; the launch traced here: 31.2 us
  Pallas kernels  27.3 us (87%)
  local copies, waits for them, and re-layouts  3.31 us (11%)
  between operations  0.64 us (2%)
    pallas_call x1, Pallas kernels, body(): pl.pallas_call(functools.partial(fused_kernel, counts), out_shape=(jax.Sh...  27.3 us
    unnamed x2, local copies, waits for them, and re-layouts  3.31 us

profile of v5, /device:TPU:0, one launch (start us, length us, event | category | flops | bytes accessed | tf_op | source)
XLA Modules:
  0.0 31.2 jit_solution(16862665168051056210)
XLA Ops:
  0.6 27.3 %shard_map.77 = (f32[3,2,32,128]{3,2,1,0:T(8,128)}, f32[3,128,256]{2,1,0:T(8,128)}) custom-call(f32[3,3,3]{2,1,0:T(4,128)} %exch.1, f32[3,2,32,128]{3,2,1,0:T(8,128)} %spins_hbm.1, f32[2,2,32,128]{3,2,1,0:T(8,128)} %unif_hbm.1, f32[2,3,2,32,128]{4,3,2,1,0:T(8,128)} %trial_hbm.1, f32[3,128,256]{2,1,0:T(8,128)} %film_hbm.1, f32[128,256]{1,0:T(8,128)} %anis_hbm.1), custom_call_target="tpu_custom_call" | custom-call | tf_op jit(solution)/shard_map/pallas_call | solution.py:780
  27.9 1.5 %copy.10 = f32[3,2,32,128]{3,2,1,0:T(8,128)} copy(f32[3,2,32,128]{3,2,1,0:T(8,128)} %get-tuple-element.4) | data formatting | bytes 196608
  29.5 1.8 %copy.11 = f32[3,128,256]{2,1,0:T(8,128)} copy(f32[3,128,256]{2,1,0:T(8,128)} %get-tuple-element.5) | data formatting | bytes 786432
